TPU v7x, 32 devices: a whole 2x2x4 slice. The times are simulated.
32 devices in a mesh: groups: 2 (over y), tensor: 4 (over z), dp: 4 (over x, core).
Axes of the slice: x: 2, y: 2, z: 4, core: 2. Of those that a mesh axis runs over, the one named last changes fastest.
Arguments:
- gen_states: bfloat16 [64, 64, 8192], P(('groups', 'dp'), None, 'tensor'), parts along dimension 0, may hold values from -6 to 6
- lengths: int32 [64], P('groups'), parts along dimension 0, may hold values from 1 to 64
- route: int32 [64], P('groups'), parts along dimension 0, may hold values from 0 to 3, as said below
- ln_gain: float32 [8192], replicated, may hold values from 0.5 to 1.5
- w_query: bfloat16 [8192, 4096], P('dp', 'tensor'), may hold values from -1 to 1
- w_keyval: bfloat16 [4, 8192, 256], P(None, 'dp'), may hold values from -1 to 1
- w_out: bfloat16 [4096, 8192], P('tensor', 'dp'), may hold values from -0.125 to 0.125
- w_score: bfloat16 [3, 8192], P(None, 'tensor'), may hold values from -0.0625 to 0.0625
Outputs:
- reward_states: bfloat16 [64, 64, 8192], P(('groups', 'dp'), None, 'tensor'), parts along dimension 0
- scores: float32 [64, 3], P(('groups', 'dp')), parts along dimension 0
There are 2 independent parts, one for each index of `groups`. A program takes and returns all parts, laid end to end along the dimension named above; an argument that names none is the same for every part. Nothing has to cross between parts.
Inputs may be any that keep to these rules, and one draw needn't show every extreme that they name: `route`: from each generator device (aligned blocks of 8 responses) exactly 2 responses go to each of 4 distinct reward devices, and every reward device receives exactly 8 responses.
All inputs are finite; a program needn't handle non-finite values.
Results may differ from a plain program's by a relative error of at most 0.0095.
The roundings to bfloat16 on the way count: a program that leaves them out, or rounds other values in their place, can miss the bound.
Values may be sent and summed in bfloat16 or wider, within the bound.
A program may use at most 192 MiB of HBM per device.

v0:
```python
import math

import jax
import jax.numpy as jnp
from jax import lax
from jax.sharding import PartitionSpec as P

D = 8192
HD = 128
QH = 32
KVH = 4
OBJ = 3
CAP = 2


EPS = 1e-05
THETA = 500000.0


def rotary_tables(row_count, period, head_size):
    positions = (jnp.arange(row_count, dtype=jnp.int32) % period).astype(jnp.float32)
    half_size = head_size // 2
    exponents = jnp.arange(half_size, dtype=jnp.float32) * (2.0 / head_size)
    inverse = jnp.power(jnp.float32(THETA), -exponents)
    angles = positions[:, None] * inverse[None, :]
    return (jnp.cos(angles), jnp.sin(angles))


def rotate(entries, cosine_table, sine_table):
    half_size = entries.shape[-1] // 2
    leading = entries[..., :half_size]
    back_part = entries[..., half_size:]
    return jnp.concatenate(
        [
            leading * cosine_table - back_part * sine_table,
            back_part * cosine_table + leading * sine_table,
        ],
        axis=-1,
    )


def body(gen_states, lengths, route, ln_gain, w_query, w_keyval, w_out, w_score):
    dp_count = lax.axis_size("dp")
    dp_index = lax.axis_index("dp")
    tensor_index = lax.axis_index("tensor")
    resp_dev, slot_len, width_part = gen_states.shape
    heads_here = w_query.shape[1] // HD
    row_count = resp_dev * slot_len
    route_table = route.reshape(dp_count, resp_dev)
    my_routes = lax.dynamic_index_in_dim(route_table, dp_index, 0, keepdims=False)
    slot_ids = jnp.arange(resp_dev, dtype=jnp.int32)
    earlier = slot_ids[None, :] < slot_ids[:, None]
    same_target = my_routes[:, None] == my_routes[None, :]
    sender_ranks = jnp.sum((earlier & same_target).astype(jnp.int32), axis=1)
    device_ids = jnp.arange(dp_count, dtype=jnp.int32)
    capacity_ids = jnp.arange(CAP, dtype=jnp.int32)
    select = (my_routes[None, None, :] == device_ids[:, None, None]) & (
        sender_ranks[None, None, :] == capacity_ids[None, :, None]
    )
    select = select.reshape(dp_count * CAP, resp_dev)
    outgoing = jnp.dot(
        select.astype(jnp.bfloat16),
        gen_states.reshape(resp_dev, slot_len * width_part),
        preferred_element_type=jnp.float32,
    ).astype(jnp.bfloat16)
    arrived = lax.all_to_all(
        outgoing.reshape(dp_count, CAP, slot_len * width_part),
        "dp",
        split_axis=0,
        concat_axis=0,
        tiled=True,
    )
    arrivals = route_table == dp_index
    counts = jnp.sum(arrivals.astype(jnp.int32), axis=1)
    offsets = jnp.cumsum(counts) - counts
    reward_ids = jnp.arange(resp_dev, dtype=jnp.int32)
    placing = (
        reward_ids[:, None, None] == offsets[None, :, None] + capacity_ids[None, None, :]
    ) & (capacity_ids[None, None, :] < counts[None, :, None])
    placing = placing.reshape(resp_dev, dp_count * CAP)
    states = jnp.dot(
        placing.astype(jnp.bfloat16),
        arrived.reshape(dp_count * CAP, slot_len * width_part),
        preferred_element_type=jnp.float32,
    ).astype(jnp.bfloat16)
    flat_arrivals = arrivals.reshape(-1).astype(jnp.int32)
    places = jnp.cumsum(flat_arrivals) - 1
    owners = (places[None, :] == reward_ids[:, None]) & (flat_arrivals[None, :] == 1)
    reward_lengths = jnp.sum(jnp.where(owners, lengths[None, :], 0), axis=1)
    local_rows = states.reshape(row_count, width_part)
    full_rows = lax.all_gather(local_rows, "tensor", axis=1, tiled=True)
    full_float = full_rows.astype(jnp.float32)
    mean_square = jnp.mean(full_float * full_float, axis=1, keepdims=True)
    normed = (full_float * lax.rsqrt(mean_square + EPS) * ln_gain[None, :]).astype(jnp.bfloat16)
    kv_index = tensor_index * heads_here // (QH // KVH)
    kv_weight = lax.dynamic_index_in_dim(w_keyval, kv_index, 0, keepdims=False)

    def project(shard_piece):
        return jnp.dot(normed, shard_piece, preferred_element_type=jnp.float32)

    queries = project(lax.all_gather(w_query, "dp", axis=0, tiled=True))
    keyval = project(lax.all_gather(kv_weight, "dp", axis=0, tiled=True))
    cosine_table, sine_table = rotary_tables(row_count, slot_len, HD)
    queries = rotate(
        queries.reshape(row_count, heads_here, HD), cosine_table[:, None, :], sine_table[:, None, :]
    ).astype(jnp.bfloat16)
    key_rows = rotate(keyval[:, :HD], cosine_table, sine_table).astype(jnp.bfloat16)
    value_rows = keyval[:, HD:].astype(jnp.bfloat16)
    per_block = min(resp_dev, max(1, 512 // slot_len))
    block_rows = per_block * slot_len
    block_count = resp_dev // per_block
    row_ids = jnp.arange(block_rows, dtype=jnp.int32)
    allowed = (row_ids[:, None] >= row_ids[None, :]) & (
        row_ids[:, None] // slot_len == row_ids[None, :] // slot_len
    )
    score_scale = 1.0 / math.sqrt(HD)

    def attend(block_in):
        query_block, key_block, value_block = block_in
        scores = (
            jnp.einsum("qhd,kd->hqk", query_block, key_block, preferred_element_type=jnp.float32)
            * score_scale
        )
        scores = jnp.where(allowed[None], scores, -1e30)
        row_peak = jnp.max(scores, axis=2, keepdims=True)
        weights = jnp.exp(scores - row_peak)
        weights = (weights / jnp.sum(weights, axis=2, keepdims=True)).astype(jnp.bfloat16)
        mixture = jnp.einsum(
            "hqk,kd->qhd", weights, value_block, preferred_element_type=jnp.float32
        )
        return mixture.astype(jnp.bfloat16)

    attended = lax.map(
        attend,
        (
            queries.reshape(block_count, block_rows, heads_here, HD),
            key_rows.reshape(block_count, block_rows, HD),
            value_rows.reshape(block_count, block_rows, HD),
        ),
    )
    attended = attended.reshape(row_count, heads_here * HD)
    partial_value = jnp.dot(
        attended,
        lax.all_gather(w_out, "dp", axis=1, tiled=True),
        preferred_element_type=jnp.float32,
    )
    summed = lax.psum_scatter(
        partial_value.astype(jnp.bfloat16), "tensor", scatter_dimension=1, tiled=True
    ).astype(jnp.float32)
    positions = jnp.arange(row_count, dtype=jnp.int32) % slot_len
    validity = (positions < jnp.repeat(reward_lengths, slot_len)).astype(jnp.float32)
    reward_flat = ((local_rows.astype(jnp.float32) + summed) * validity[:, None]).astype(
        jnp.bfloat16
    )
    last_index = reward_ids * slot_len + reward_lengths - 1
    last_rows = jnp.take(reward_flat, last_index, axis=0)
    last_float = last_rows.astype(jnp.float32)
    local_dots = jnp.dot(last_rows, w_score.T, preferred_element_type=jnp.float32)
    local_squares = jnp.sum(last_float * last_float, axis=1, keepdims=True)
    head_dots, square_sum = lax.psum((local_dots, local_squares), "tensor")
    reward_scores = head_dots * lax.rsqrt(square_sum / D + EPS)
    returning = jnp.dot(
        placing.T.astype(jnp.float32), reward_scores, precision=lax.Precision.HIGHEST
    ).reshape(dp_count, CAP, OBJ)
    homecoming = lax.all_to_all(returning, "dp", split_axis=0, concat_axis=0, tiled=True)
    scores = jnp.dot(
        select.T.astype(jnp.float32),
        homecoming.reshape(dp_count * CAP, OBJ),
        precision=lax.Precision.HIGHEST,
    )
    return (reward_flat.reshape(resp_dev, slot_len, width_part), scores)


def solution(mesh):
    in_specs = (
        P(("groups", "dp"), None, "tensor"),
        P("groups"),
        P("groups"),
        P(),
        P("dp", "tensor"),
        P(None, "dp", None),
        P("tensor", "dp"),
        P(None, "tensor"),
    )
    out_specs = (P(("groups", "dp"), None, "tensor"), P(("groups", "dp"), None))
    return jax.shard_map(body, mesh=mesh, in_specs=in_specs, out_specs=out_specs, check_vma=False)
```

profile of v0, /device:TPU:0, one launch (start us, length us, event | category | flops | bytes accessed | tf_op | source)
XLA Modules:
  0.0 646.4 jit_solution(12684874708222639563)
XLA Ops:
  7.2 0.0 copy-start
  7.2 0.7 reshape.459
  7.9 0.2 convert_reduce_fusion
  8.2 2.7 copy.57
  10.9 0.7 convolution_convert_fusion
  11.6 2.6 reshape.463
  14.2 4.2 all-to-all-start
  18.4 0.0 all-gather.6.cloned.1.call-start
  18.4 0.1 convert_reduce_fusion.1
  18.6 0.2 reduce-window.16
  18.8 25.4 %all-to-all-done = bf16[4,2,131072]{2,1,0:T(2,128)(2,1)S(1)} async-done(((bf16[4,2,131072]{2,1,0:T(2,128)(2,1)}), bf16[4,2,131072]{2,1,0:T(2,128)(2,1)S(1)}, u32[]{:S(2)}, u32[]{:S(2)}) %all-to-all-start) | async-done | bytes 2097184 | tf_op jit(solution)/shard_map/all_to_all | solution.py:66
  44.1 4.4 fusion.1
  48.6 3.9 reshape.464
  52.5 0.0 all-gather.6.cloned.1.call-update
  52.5 0.0 all-gather.12.cloned.1.call-start
  52.5 2.3 constant_dynamic-slice_fusion
  54.8 0.0 all-gather.12.cloned.1.call-update
  54.8 0.0 all-gather.8.cloned.1.call-start
  54.9 0.7 all-gather.8.cloned.1.call-update
  55.6 0.0 all-gather.10.cloned.1.call-start
  55.6 0.5 all-gather.10.cloned.1.call-update
  56.2 0.0 reduce-scatter.2.cloned.1.call-start
  56.2 0.2 fusion.24
  56.5 0.0 copy-start.4
  56.5 147.0 %all-gather.6.cloned.1.call-done = bf16[512,8192]{1,0:T(8,128)(2,1)} async-done(((bf16[512,2048]{1,0:T(8,128)(2,1)}), bf16[512,8192]{1,0:T(8,128)(2,1)}) %all-gather.6.cloned.1.call-update) | async-done | bytes 8388624 | tf_op jit(solution)/shard_map/all_gather | solution.py:91
  203.4 5.1 fusion.2
  208.5 29.8 %all-gather.12.cloned.1.call-done = bf16[1,8192,256]{2,1,0:T(8,128)(2,1)} async-done(((bf16[1,2048,256]{2,1,0:T(8,128)(2,1)}), bf16[1,8192,256]{2,1,0:T(8,128)(2,1)}) %all-gather.12.cloned.1.call-update) | async-done | bytes 4194320 | tf_op jit(solution)/shard_map/all_gather | solution.py:102
  238.3 0.0 copy-done.4
  238.3 7.6 %fusion.6 = f32[512,256]{0,1:T(8,128)S(1)} fusion(bf16[1,8192,256]{2,1,0:T(8,128)(2,1)} %all-gather.12.cloned.1.call-done, bf16[512,8192]{1,0:T(8,128)(2,1)} %all-gather.6.cloned.1.call-done, f32[8192]{0:T(1024)S(1)} %copy-done.4, f32[512]{0:T(512)S(1)} %add_rsqrt_fusion), kind=kOutput, calls=%fused_computation.15 | convolution fusion | flops 2164260864 | bytes 13142016 | tf_op jit(solution)/shard_map/dot_general | solution.py:99
  245.9 0.6 subtract_convert_fusion.1
  246.5 0.1 copy.45
  246.6 0.1 copy.43
  246.7 99.1 %all-gather.8.cloned.1.call-done = bf16[8192,1024]{1,0:T(8,128)(2,1)} async-done(((bf16[2048,1024]{1,0:T(8,128)(2,1)}), bf16[8192,1024]{1,0:T(8,128)(2,1)}) %all-gather.8.cloned.1.call-update) | async-done | bytes 16777232 | tf_op jit(solution)/shard_map/all_gather | solution.py:101
  345.8 15.1 %fusion.16 = f32[64,8,8,128]{3,1,2,0:T(8,128)S(1)} fusion(bf16[8192,1024]{1,0:T(8,128)(2,1)} %all-gather.8.cloned.1.call-done, bf16[512,8192]{1,0:T(8,128)(2,1)} %all-gather.6.cloned.1.call-done, f32[8192]{0:T(1024)S(1)} %copy-done.4, f32[512]{0:T(512)S(1)} %add_rsqrt_fusion), kind=kOutput, calls=%fused_computation.26 | convolution fusion | flops 8606711808 | bytes 27297792 | tf_op jit(solution)/shard_map/dot_general | solution.py:99
  360.9 0.5 copy.58
  361.4 0.7 fusion.55
  362.1 0.8 subtract_convert_fusion
  362.9 1.3 fusion.20
  364.2 5.7 fusion.56
  369.9 4.1 fusion.19
  374.1 79.1 %all-gather.10.cloned.1.call-done = bf16[1024,8192]{1,0:T(8,128)(2,1)} async-done(((bf16[1024,2048]{1,0:T(8,128)(2,1)}), bf16[1024,8192]{1,0:T(8,128)(2,1)}) %all-gather.10.cloned.1.call-update) | async-done | bytes 16777232 | tf_op jit(solution)/shard_map/all_gather | solution.py:144
  453.2 16.9 %convolution_convert_fusion.1 = bf16[512,8192]{1,0:T(8,128)(2,1)} fusion(bf16[512,1024]{0,1:T(8,128)(2,1)S(1)} %bitcast.67, bf16[1024,8192]{1,0:T(8,128)(2,1)} %all-gather.10.cloned.1.call-done), kind=kOutput, calls=%fused_computation.10 | convolution fusion | flops 8594128896 | bytes 26214400 | tf_op jit(solution)/shard_map/dot_general | solution.py:142
  470.1 0.0 copy-start.2
  470.1 0.0 reduce-scatter.2.cloned.1.call-update
  470.2 0.6 copy-done.2
  470.8 0.1 copy.48
  470.9 0.1 reduce-window.17
  470.9 0.1 add_reduce_fusion
  471.0 0.0 copy-done.3
  471.0 0.1 select_reduce_fusion
  471.2 0.1 broadcast_in_dim.52
  471.2 0.1 reshape.468
  471.4 0.1 fusion.40
  471.4 143.3 %reduce-scatter.2.cloned.1.call-done = bf16[512,2048]{1,0:T(8,128)(2,1)} async-done(((bf16[512,8192]{1,0:T(8,128)(2,1)}), bf16[512,2048]{1,0:T(8,128)(2,1)}) %reduce-scatter.2.cloned.1.call-update) | async-done | bytes 2097168 | tf_op jit(solution)/shard_map/reduce_scatter | solution.py:147
  614.8 0.0 copy-done.1
  614.8 3.5 multiply_convert_fusion
  618.3 2.5 gather_fusion
  620.8 0.2 multiply_reduce_fusion
  621.0 0.0 copy-done
  621.0 0.2 fusion.29
  621.2 11.1 %all-reduce = (f32[8,3]{0,1:T(4,128)S(1)}, f32[8,1]{0,1:T(1,128)S(1)}) all-reduce(f32[8,3]{0,1:T(4,128)S(1)} %fusion.29, f32[8,1]{0,1:T(1,128)S(1)} %bitcast.65), channel_id=1, replica_groups=mesh['groups'=2,'tensor'=4,'dp'=4] {'tensor'}, use_global_device_ids=true, to_apply=%region_9.10 | all-reduce | flops 32 | bytes 256 | tf_op jit(solution)/shard_map/psum | solution.py:160
  632.3 0.1 fusion.30
  632.5 6.6 %all_to_all.10 = f32[4,2,3]{2,1,0:T(2,128)S(1)} all-to-all(f32[4,2,3]{2,1,0:T(2,128)S(1)} %fusion.30), channel_id=1, replica_groups=mesh['groups'=2,'tensor'=4,'dp'=4] {'dp'}, dimensions={0} | all-to-all | bytes 192 | tf_op jit(solution)/shard_map/all_to_all | solution.py:165
  639.0 0.8 convolution_bitcast_fusion.1
  (20 shorter events, 0.1 us)
Async XLA Ops:
  7.2 613.8 %copy-start = (bf16[3,2048]{1,0:T(4,128)(2,1)S(1)}, bf16[3,2048]{1,0:T(4,128)(2,1)}, u32[]{:S(2)}) copy-start(bf16[3,2048]{1,0:T(4,128)(2,1)} %param.15) | copy-start | bytes 36868
  14.2 29.9 %all-to-all-start = ((bf16[4,2,131072]{2,1,0:T(2,128)(2,1)}), bf16[4,2,131072]{2,1,0:T(2,128)(2,1)S(1)}, u32[]{:S(2)}, u32[]{:S(2)}) async-start(bf16[4,2,131072]{2,1,0:T(2,128)(2,1)} %reshape.463), calls=%async_computation | async-start | bytes 4194304 | tf_op jit(solution)/shard_map/all_to_all | solution.py:66
  18.4 185.0 %all-gather.6.cloned.1.call-start = ((), (), s32[]{:S(2)}) async-start(), calls=%async_computation.3 | async-start | bytes 10485760 | tf_op jit(solution)/shard_map/all_gather | solution.py:91
  52.5 185.8 %all-gather.12.cloned.1.call-start = ((), (), s32[]{:S(2)}) async-start(), calls=%async_computation.7 | async-start | bytes 5242880 | tf_op jit(solution)/shard_map/all_gather | solution.py:102
  54.8 291.0 %all-gather.8.cloned.1.call-start = ((), (), s32[]{:S(2)}) async-start(), calls=%async_computation.4 | async-start | bytes 20971520 | tf_op jit(solution)/shard_map/all_gather | solution.py:101
  55.6 397.6 %all-gather.10.cloned.1.call-start = ((), (), s32[]{:S(2)}) async-start(), calls=%async_computation.5 | async-start | bytes 20971520 | tf_op jit(solution)/shard_map/all_gather | solution.py:144
  56.2 558.6 %reduce-scatter.2.cloned.1.call-start = ((), (), s32[]{:S(2)}) async-start(), calls=%async_computation.6 | async-start | bytes 10485760 | tf_op jit(solution)/shard_map/reduce_scatter | solution.py:147
  56.5 181.8 %copy-start.4 = (f32[8192]{0:T(1024)S(1)}, f32[8192]{0:T(1024)}, u32[]{:S(2)}) copy-start(f32[8192]{0:T(1024)} %param.11) | copy-start | bytes 98308
  470.1 0.7 copy-start.2
  470.1 0.9 copy-start.3
  470.1 144.7 %copy-start.1 = (bf16[512,2048]{1,0:T(8,128)(2,1)S(1)}, bf16[512,2048]{1,0:T(8,128)(2,1)}, u32[]{:S(2)}) copy-start(bf16[512,2048]{1,0:T(8,128)(2,1)} %reshape.464) | copy-start | bytes 6291460
Sparse Core Ops, SparseCore 0:
  52.6 150.7 all-gather.5
  205.6 32.6 all-gather.11
  239.8 105.9 all-gather.7
  347.2 105.9 all-gather.9
  470.3 144.4 reduce-scatter.1
where the time goes:
time: 647 us; the launch traced here: 646 us
  waiting for transfers between devices  525 us (81%)
  matrix products  51.3 us (8%)
  blocking collectives  17.7 us (3%)
  other arithmetic  17.1 us (3%)
  local copies, waits for them, and re-layouts  17 us (3%)
  between operations  14 us (2%)
    all_gather x1, waiting for transfers between devices, body(): full_rows = lax.all_gather(local_rows, 'tensor', axis=1, tiled=True)  147 us
    reduce_scatter x1, waiting for transfers between devices, body(): lax.psum_scatter(partial_value.astype(jnp.bfloat16), 'tensor', scatter_di...  143 us
    all_gather x1, waiting for transfers between devices, body(): queries = project(lax.all_gather(w_query, 'dp', axis=0, tiled=True))  99.1 us
    all_gather x1, waiting for transfers between devices, body(): lax.all_gather(w_out, 'dp', axis=1, tiled=True)  79.1 us
    all_gather x1, waiting for transfers between devices, body(): keyval = project(lax.all_gather(kv_weight, 'dp', axis=0, tiled=True))  29.8 us
    all_to_all x1, waiting for transfers between devices, body(): lax.all_to_all(outgoing.reshape(dp_count, CAP, slot_len * width_part), 'd...  25.4 us
    dot_general x2, matrix products, project(): return jnp.dot(normed, shard_piece, preferred_element_type=jnp.float32)  22.7 us
    dot_general x1, matrix products, body(): jnp.dot(attended, lax.all_gather(w_out, 'dp', axis=1, tiled=True), prefer...  16.9 us
  transfers between devices with their start and end apart: 6, of which 6 were waited for; matrix products, arithmetic and copies ran while one was open for 7% of the time, Pallas kernels for 0%

commit v1 on v0

v1 whole, which is shorter than its diff:
```python
import functools
import math

import jax
import jax.numpy as jnp
from jax import lax
from jax.experimental import pallas as pl
from jax.experimental.pallas import tpu as pltpu
from jax.sharding import PartitionSpec as P

D = 8192
HD = 128
QH = 32
KVH = 4
OBJ = 3
CAP = 2
CHUNKS = 2

EPS = 1e-05
THETA = 500000.0


def rotary_tables(row_count, period, head_size):
    positions = (jnp.arange(row_count, dtype=jnp.int32) % period).astype(jnp.float32)
    half_size = head_size // 2
    exponents = jnp.arange(half_size, dtype=jnp.float32) * (2.0 / head_size)
    inverse = jnp.power(jnp.float32(THETA), -exponents)
    angles = positions[:, None] * inverse[None, :]
    return (jnp.cos(angles), jnp.sin(angles))


def attention_kernel(heads, slot_len, q_ref, kv_ref, cos_ref, sin_ref, out_ref):
    rows = q_ref.shape[0]
    cosine, sine = cos_ref[...], sin_ref[...]

    def turn(x):
        return (x * cosine + pltpu.roll(x, HD // 2, 1) * sine).astype(jnp.bfloat16)

    key = turn(kv_ref[:, :HD])
    value = kv_ref[:, HD:].astype(jnp.bfloat16)
    row_ids = lax.broadcasted_iota(jnp.int32, (rows, rows), 0)
    key_ids = lax.broadcasted_iota(jnp.int32, (rows, rows), 1)
    allowed = (row_ids >= key_ids) & (row_ids // slot_len == key_ids // slot_len)
    for head in range(heads):
        query = turn(q_ref[:, head * HD:(head + 1) * HD])
        scores = lax.dot_general(
            query, key, (((1,), (1,)), ((), ())), preferred_element_type=jnp.float32
        ) * (1.0 / math.sqrt(HD))
        scores = jnp.where(allowed, scores, -1e30)
        weights = jnp.exp(scores - jnp.max(scores, axis=1, keepdims=True))
        weights = (weights / jnp.sum(weights, axis=1, keepdims=True)).astype(jnp.bfloat16)
        mixed = jnp.dot(weights, value, preferred_element_type=jnp.float32)
        out_ref[:, head * HD:(head + 1) * HD] = mixed.astype(jnp.bfloat16)


def attention(queries, keyval, cosine, sine, slot_len):
    row_count, width = queries.shape
    step = 2 * slot_len
    row_block = lambda i: (i, 0)
    return pl.pallas_call(
        functools.partial(attention_kernel, width // HD, slot_len),
        grid=(row_count // step,),
        in_specs=[
            pl.BlockSpec((step, width), row_block),
            pl.BlockSpec((step, 2 * HD), row_block),
            pl.BlockSpec((step, HD), lambda i: (0, 0)),
            pl.BlockSpec((step, HD), lambda i: (0, 0)),
        ],
        out_specs=pl.BlockSpec((step, width), row_block),
        out_shape=jax.ShapeDtypeStruct((row_count, width), jnp.bfloat16),
        cost_estimate=pl.CostEstimate(
            flops=row_count * step * width * 4,
            bytes_accessed=row_count * width * 6,
            transcendentals=row_count * step * width // HD,
        ),
    )(queries, keyval, cosine, sine)


def gather_dp(shard, axis):
    n = lax.axis_size("dp")
    groups = lax.axis_size("groups")
    me, group = lax.axis_index("dp"), lax.axis_index("groups")
    extent = shard.shape[axis]
    part = extent // groups
    shape = list(shard.shape)
    shape[axis] = n * extent
    full = jnp.zeros(shape, shard.dtype)

    def put(full, piece, start):
        where = [0] * len(shape)
        where[axis] = start
        return lax.dynamic_update_slice(full, piece, where)

    swap = [(i, i ^ 1) for i in range(n)]
    mine = lax.dynamic_slice_in_dim(shard, group * part, part, axis)
    pieces = []
    for chip in range(1, n // 2):
        far = lax.ppermute(mine, "dp", [(i, (i + 2 * chip) % n) for i in range(n)])
        source = (me - 2 * chip + n) % n
        pieces.append((far, source, group))
        for other in range(1, groups):
            passed = lax.ppermute(
                far, "groups", [(g, (g + other) % groups) for g in range(groups)]
            )
            pieces.append((passed, source, (group - other + groups) % groups))
    full = put(full, shard, me * extent)
    full = put(full, lax.ppermute(shard, "dp", swap), (me ^ 1) * extent)
    for piece, source, which in pieces:
        full = put(full, piece, source * extent + which * part)
        full = put(
            full, lax.ppermute(piece, "dp", swap), (source ^ 1) * extent + which * part
        )
    return full


def gather_line(block):
    count = lax.axis_size("tensor")
    up = [(i, i + 1) for i in range(count - 1)]
    down = [(i + 1, i) for i in range(count - 1)]
    rising, falling = [block], [block]
    for _ in range(count - 1):
        rising.append(lax.ppermute(rising[-1], "tensor", up))
        falling.append(lax.ppermute(falling[-1], "tensor", down))
    mine = lax.axis_index("tensor")
    return [block] + [
        jnp.where(mine >= s, rising[s], falling[count - s]) for s in range(1, count)
    ]


def sum_line(partial):
    count = lax.axis_size("tensor")
    mine = lax.axis_index("tensor")
    width = partial.shape[1] // count
    up = [(i, i + 1) for i in range(count - 1)]
    down = [(i + 1, i) for i in range(count - 1)]

    def block(index):
        index = jnp.clip(index, 0, count - 1)
        return lax.dynamic_slice_in_dim(partial, index * width, width, 1)

    rising = falling = None
    for step in range(count - 1):
        upward = block(mine + (count - 1 - step))
        downward = block(mine - (count - 1 - step))
        if step:
            upward = (upward.astype(jnp.float32) + rising.astype(jnp.float32)).astype(jnp.bfloat16)
            downward = (downward.astype(jnp.float32) + falling.astype(jnp.float32)).astype(jnp.bfloat16)
        rising = lax.ppermute(upward, "tensor", up)
        falling = lax.ppermute(downward, "tensor", down)
    return (
        block(mine).astype(jnp.float32)
        + rising.astype(jnp.float32)
        + falling.astype(jnp.float32)
    )


def body(gen_states, lengths, route, ln_gain, w_query, w_keyval, w_out, w_score):
    n = lax.axis_size("dp")
    me = lax.axis_index("dp")
    tensor_count = lax.axis_size("tensor")
    tensor_index = lax.axis_index("tensor")
    resp_dev, slot_len, width_part = gen_states.shape
    heads_here = w_query.shape[1] // HD
    row_count = resp_dev * slot_len
    route_table = route.reshape(n, resp_dev)
    my_routes = lax.dynamic_index_in_dim(route_table, me, 0, keepdims=False)
    slot_ids = jnp.arange(resp_dev, dtype=jnp.int32)
    earlier = slot_ids[None, :] < slot_ids[:, None]
    same_target = my_routes[:, None] == my_routes[None, :]
    sender_ranks = jnp.sum((earlier & same_target).astype(jnp.int32), axis=1)
    device_ids = jnp.arange(n, dtype=jnp.int32)
    capacity_ids = jnp.arange(CAP, dtype=jnp.int32)
    select = (my_routes[None, None, :] == device_ids[:, None, None]) & (
        sender_ranks[None, None, :] == capacity_ids[None, :, None]
    )
    picks = jnp.sum(jnp.where(select, slot_ids[None, None, :], 0), axis=2)
    arrivals = route_table == me
    counts = jnp.sum(arrivals.astype(jnp.int32), axis=1)
    offsets = jnp.cumsum(counts) - counts
    states = jnp.zeros((resp_dev + CAP, slot_len, width_part), gen_states.dtype)
    for shift in range(n):
        target = (me + shift) % n
        pair = jnp.concatenate(
            [
                lax.dynamic_slice_in_dim(gen_states, picks[target, j], 1, 0)
                for j in range(CAP)
            ],
            axis=0,
        )
        if shift:
            pair = lax.ppermute(pair, "dp", [(i, (i + shift) % n) for i in range(n)])
        source = (me - shift + n) % n
        start = jnp.where(counts[source] > 0, offsets[source], resp_dev)
        states = lax.dynamic_update_slice_in_dim(states, pair, start, 0)

    reward_ids = slot_ids
    placing = (
        reward_ids[:, None, None] == offsets[None, :, None] + capacity_ids[None, None, :]
    ) & (capacity_ids[None, None, :] < counts[None, :, None])
    placing = placing.reshape(resp_dev, n * CAP)
    flat_arrivals = arrivals.reshape(-1).astype(jnp.int32)
    places = jnp.cumsum(flat_arrivals) - 1
    owners = (places[None, :] == reward_ids[:, None]) & (flat_arrivals[None, :] == 1)
    reward_lengths = jnp.sum(jnp.where(owners, lengths[None, :], 0), axis=1)

    kv_index = tensor_index * heads_here // (QH // KVH)
    kv_shard = lax.dynamic_index_in_dim(w_keyval, kv_index, 0, keepdims=False)
    kv_full = gather_dp(kv_shard, 0)
    query_full = gather_dp(w_query, 0)
    out_full = gather_dp(w_out, 1)

    cosine, sine = rotary_tables(2 * slot_len, slot_len, HD)
    cosine = jnp.concatenate([cosine, cosine], axis=1)
    sine = jnp.concatenate([-sine, sine], axis=1)

    resp_chunk = resp_dev // CHUNKS
    rows_chunk = resp_chunk * slot_len
    outputs = []
    for chunk in range(CHUNKS):
        low = chunk * resp_chunk
        local = states[low:low + resp_chunk].reshape(rows_chunk, width_part)
        blocks = gather_line(local)
        full = jnp.zeros((rows_chunk, tensor_count * width_part), local.dtype)
        for s, piece in enumerate(blocks):
            owner = (tensor_index - s + tensor_count) % tensor_count
            full = lax.dynamic_update_slice_in_dim(full, piece, owner * width_part, 1)
        wide = full.astype(jnp.float32)
        mean_square = jnp.mean(wide * wide, axis=1, keepdims=True)
        normed = (wide * lax.rsqrt(mean_square + EPS) * ln_gain[None, :]).astype(jnp.bfloat16)
        queries = jnp.dot(normed, query_full, preferred_element_type=jnp.float32)
        keyval = jnp.dot(normed, kv_full, preferred_element_type=jnp.float32)
        attended = attention(queries, keyval, cosine, sine, slot_len)
        partial = jnp.dot(attended, out_full, preferred_element_type=jnp.float32)
        summed = sum_line(partial.astype(jnp.bfloat16))
        positions = jnp.arange(rows_chunk, dtype=jnp.int32) % slot_len
        valid = positions < jnp.repeat(reward_lengths[low:low + resp_chunk], slot_len)
        outputs.append(
            (
                (local.astype(jnp.float32) + summed) * valid.astype(jnp.float32)[:, None]
            ).astype(jnp.bfloat16)
        )
    reward_flat = jnp.concatenate(outputs, axis=0)

    last_index = reward_ids * slot_len + reward_lengths - 1
    last_rows = jnp.take(reward_flat, last_index, axis=0)
    last_float = last_rows.astype(jnp.float32)
    local_dots = jnp.dot(last_rows, w_score.T, preferred_element_type=jnp.float32)
    local_squares = jnp.sum(last_float * last_float, axis=1, keepdims=True)
    head_dots, square_sum = lax.psum((local_dots, local_squares), "tensor")
    reward_scores = head_dots * lax.rsqrt(square_sum / D + EPS)
    returning = jnp.dot(
        placing.T.astype(jnp.float32), reward_scores, precision=lax.Precision.HIGHEST
    ).reshape(n, CAP, OBJ)
    homecoming = lax.all_to_all(returning, "dp", split_axis=0, concat_axis=0, tiled=True)
    scores = jnp.dot(
        select.reshape(n * CAP, resp_dev).T.astype(jnp.float32),
        homecoming.reshape(n * CAP, OBJ),
        precision=lax.Precision.HIGHEST,
    )
    return (reward_flat.reshape(resp_dev, slot_len, width_part), scores)


def solution(mesh):
    in_specs = (
        P(("groups", "dp"), None, "tensor"),
        P("groups"),
        P("groups"),
        P(),
        P("dp", "tensor"),
        P(None, "dp", None),
        P("tensor", "dp"),
        P(None, "tensor"),
    )
    out_specs = (P(("groups", "dp"), None, "tensor"), P(("groups", "dp"), None))
    return jax.shard_map(body, mesh=mesh, in_specs=in_specs, out_specs=out_specs, check_vma=False)
```

time: 647 us -> 582 us (0.90); the launches traced: 646 us -> 574 us
  waiting for transfers between devices: 525 us -> 271 us
  starting transfers between devices: 4.37 us -> 86.2 us
  local copies, waits for them, and re-layouts: 17 us -> 77.2 us
  other arithmetic: 17.1 us -> 35.5 us
  Pallas kernels: 0 us -> 15 us
  between operations: 14 us -> 22.1 us
    all_gather x4 -> x0, waiting for transfers between devices: 355 us -> none  [the longest x1 147 us: body(): full_rows = lax.all_gather(local_rows, 'tensor', axis=1, tiled=True)]
    ppermute x0 -> x42, waiting for transfers between devices: none -> 271 us  [the longest x3 75.6 us: gather_dp(): lax.ppermute(far, 'groups', [(g, (g + other) % groups) for g in range(gro...]
    reduce_scatter x1 -> x0, waiting for transfers between devices: 143 us -> none  [body(): lax.psum_scatter(partial_value.astype(jnp.bfloat16), 'tensor', scatter_di...]
    ppermute x0 -> x42, starting transfers between devices: none -> 86.2 us  [the longest x6 30.7 us: sum_line(): rising = lax.ppermute(upward, 'tensor', up)]
    dynamic_update_slice x0 -> x23, local copies, waits for them, and re-layouts: none -> 43.3 us  [the longest x18 39.5 us: put(): return lax.dynamic_update_slice(full, piece, where)]
    all_to_all x1 -> x0, waiting for transfers between devices: 25.4 us -> none  [body(): lax.all_to_all(outgoing.reshape(dp_count, CAP, slot_len * width_part), 'd...]
    convert_element_type x2 -> x9, other arithmetic: 3.54 us -> 23.8 us  [the longest x4 13.6 us: sum_line(): (upward.astype(jnp.float32) + rising.astype(jnp.float32)).astype(jnp.bflo...]
    pallas_call x0 -> x2, Pallas kernels: none -> 15 us  [attention(): pl.pallas_call(functools.partial(attention_kernel, width // HD, slot_len)...]
  transfers between devices with their start and end apart: 6 -> 42, of which waited for: 6 -> 17; matrix products, arithmetic and copies ran while one was open for 7% -> 23% of each run, Pallas kernels for 0% -> 3%
where the time goes in v1:
time: 582 us; the launch traced here: 574 us
  waiting for transfers between devices  271 us (47%)
  starting transfers between devices  86.2 us (15%)
  local copies, waits for them, and re-layouts  77.2 us (13%)
  matrix products  50.5 us (9%)
  other arithmetic  35.5 us (6%)
  between operations  22.1 us (4%)
  blocking collectives  16.2 us (3%)
  Pallas kernels  15 us (3%)
    ppermute x3, waiting for transfers between devices, gather_dp(): lax.ppermute(far, 'groups', [(g, (g + other) % groups) for g in range(gro...  75.6 us
    ppermute x6, waiting for transfers between devices, gather_line(): falling.append(lax.ppermute(falling[-1], 'tensor', down))  64.9 us
    ppermute x6, waiting for transfers between devices, sum_line(): falling = lax.ppermute(downward, 'tensor', down)  51.6 us
    ppermute x6, waiting for transfers between devices, sum_line(): rising = lax.ppermute(upward, 'tensor', up)  40.9 us
    dynamic_update_slice x18, local copies, waits for them, and re-layouts, put(): return lax.dynamic_update_slice(full, piece, where)  39.5 us
    ppermute x6, starting transfers between devices, sum_line(): rising = lax.ppermute(upward, 'tensor', up)  30.7 us
    ppermute x6, starting transfers between devices, gather_line(): rising.append(lax.ppermute(rising[-1], 'tensor', up))  28.9 us
    ppermute x3, waiting for transfers between devices, gather_dp(): far = lax.ppermute(mine, 'dp', [(i, (i + 2 * chip) % n) for i in range(n)])  28.9 us
  transfers between devices with their start and end apart: 42, of which 17 were waited for; matrix products, arithmetic and copies ran while one was open for 23% of the time, Pallas kernels for 3%

profile of v1, /device:TPU:0, one launch (start us, length us, event | category | flops | bytes accessed | tf_op | source)
XLA Modules:
  0.0 573.8 jit_solution(17903041462177073267)
XLA Ops:
  19.9 2.6 collective-permute-start.1
  36.1 9.2 %collective-permute-done.2 = bf16[2,64,2048]{2,1,0:T(8,128)(2,1)S(1)} collective-permute-done((bf16[2,64,2048]{2,1,0:T(8,128)(2,1)S(1)}, bf16[2,64,2048]{2,1,0:T(8,128)(2,1)S(1)}, u32[]{:S(2)}, u32[]{:S(2)}) %collective-permute-start.2) | collective-permute-done | bytes 524320 | tf_op jit(solution)/shard_map/ppermute | solution.py:191
  49.1 2.2 broadcast_in_dim.49
  51.4 2.7 constant_dynamic-update-slice_fusion.12
  55.5 2.3 collective-permute-start.15
  59.3 2.1 broadcast_in_dim.48
  62.0 7.8 %collective-permute-done.15 = bf16[1024,256]{1,0:T(8,128)(2,1)S(1)} collective-permute-done((bf16[1024,256]{1,0:T(8,128)(2,1)S(1)}, bf16[1024,256]{1,0:T(8,128)(2,1)S(1)}, u32[]{:S(2)}, u32[]{:S(2)}) %collective-permute-start.15) | collective-permute-done | bytes 524320 | tf_op jit(solution)/shard_map/ppermute | solution.py:98
  69.8 5.3 collective-permute-start.3
  80.5 5.5 collective-permute-start.30
  86.0 12.3 %collective-permute-done.31 = bf16[256,2048]{1,0:T(8,128)(2,1)} collective-permute-done((bf16[256,2048]{1,0:T(8,128)(2,1)S(1)}, bf16[256,2048]{1,0:T(8,128)(2,1)}, u32[]{:S(2)}, u32[]{:S(2)}) %collective-permute-start.31) | collective-permute-done | bytes 1048608 | tf_op jit(solution)/shard_map/ppermute | solution.py:123
  101.1 6.0 %broadcast_in_dim.50 = bf16[1024,8192]{1,0:T(8,128)(2,1)} broadcast(bf16[]{:T(256)} %constant.219.clone.1), dimensions={} | broadcast | bytes 16777218 | tf_op jit(solution)/shard_map/broadcast_in_dim | solution.py:87
  107.1 2.2 constant_dynamic-update-slice_fusion.6
  110.1 4.6 collective-permute-start.7
  114.7 6.1 %collective-permute-done.5 = bf16[256,2048]{1,0:T(8,128)(2,1)} collective-permute-done((bf16[256,2048]{1,0:T(8,128)(2,1)}, bf16[256,2048]{1,0:T(8,128)(2,1)}, u32[]{:S(2)}, u32[]{:S(2)}) %collective-permute-start.5) | collective-permute-done | bytes 1048608 | tf_op jit(solution)/shard_map/ppermute | solution.py:123
  124.1 4.9 collective-permute-start.34
  129.0 14.2 %collective-permute-done.32 = bf16[256,2048]{1,0:T(8,128)(2,1)} collective-permute-done((bf16[256,2048]{1,0:T(8,128)(2,1)}, bf16[256,2048]{1,0:T(8,128)(2,1)}, u32[]{:S(2)}, u32[]{:S(2)}) %collective-permute-start.32) | collective-permute-done | bytes 1048608 | tf_op jit(solution)/shard_map/ppermute | solution.py:123
  147.3 1.9 constant_dynamic-update-slice_fusion.8
  151.1 14.5 %collective-permute-done.6 = bf16[256,2048]{1,0:T(8,128)(2,1)S(1)} collective-permute-done((bf16[256,2048]{1,0:T(8,128)(2,1)}, bf16[256,2048]{1,0:T(8,128)(2,1)S(1)}, u32[]{:S(2)}, u32[]{:S(2)}) %collective-permute-start.6) | collective-permute-done | bytes 1048608 | tf_op jit(solution)/shard_map/ppermute | solution.py:123
  166.0 4.8 collective-permute-start.35
  170.8 17.1 %collective-permute-done.33 = bf16[256,2048]{1,0:T(8,128)(2,1)S(1)} collective-permute-done((bf16[256,2048]{1,0:T(8,128)(2,1)}, bf16[256,2048]{1,0:T(8,128)(2,1)S(1)}, u32[]{:S(2)}, u32[]{:S(2)}) %collective-permute-start.33) | collective-permute-done | bytes 1048608 | tf_op jit(solution)/shard_map/ppermute | solution.py:123
  187.9 3.9 collective-permute-start.8
  195.5 21.1 %collective-permute-done.20 = bf16[1024,1024]{1,0:T(8,128)(2,1)} collective-permute-done((bf16[1024,1024]{1,0:T(8,128)(2,1)S(1)}, bf16[1024,1024]{1,0:T(8,128)(2,1)}, u32[]{:S(2)}, u32[]{:S(2)}) %collective-permute-start.20) | collective-permute-done | bytes 2097184 | tf_op jit(solution)/shard_map/ppermute | solution.py:98
  218.7 2.4 select_dynamic-update-slice_fusion
  223.0 5.1 fusion.10.kv_ref
  228.1 2.0 copy-done.11
  230.1 35.2 %collective-permute-done.12 = bf16[1024,1024]{1,0:T(8,128)(2,1)} collective-permute-done((bf16[1024,1024]{1,0:T(8,128)(2,1)}, bf16[1024,1024]{1,0:T(8,128)(2,1)}, u32[]{:S(2)}, u32[]{:S(2)}) %collective-permute-start.12) | collective-permute-done | bytes 2097184 | tf_op jit(solution)/shard_map/ppermute | solution.py:102
  265.4 4.2 fusion.6.kv_ref
  269.6 40.3 %collective-permute-done.22 = bf16[1024,1024]{1,0:T(8,128)(2,1)} collective-permute-done((bf16[1024,1024]{1,0:T(8,128)(2,1)}, bf16[1024,1024]{1,0:T(8,128)(2,1)}, u32[]{:S(2)}, u32[]{:S(2)}) %collective-permute-start.22) | collective-permute-done | bytes 2097184 | tf_op jit(solution)/shard_map/ppermute | solution.py:102
  310.0 2.7 constant_dynamic-update-slice_fusion.17
  318.4 4.7 constant_dynamic-update-slice_fusion.5
  323.1 3.1 constant_dynamic-update-slice_fusion.4
  326.2 3.2 constant_dynamic-update-slice_fusion.3
  329.4 3.1 constant_dynamic-update-slice_fusion.2
  334.4 6.5 %fusion.12.q_ref = f32[256,1024]{1,0:T(8,128)} fusion(bf16[8192,1024]{1,0:T(8,128)(2,1)S(1)} %constant_dynamic-update-slice_fusion.13, bf16[256,8192]{1,0:T(8,128)(2,1)S(1)} %get-tuple-element.50, f32[8192]{0:T(1024)S(1)} %copy-done.22, f32[256]{0:T(256)S(1)} %add_rsqrt_fusion.1), kind=kOutput, calls=%fused_computation.27 | convolution fusion | flops 4303355904 | bytes 22053888 | tf_op jit(solution)/shard_map/dot_general | solution.py:230
  340.9 7.5 %shard_map.95 = bf16[256,1024]{1,0:T(8,128)(2,1)} custom-call(f32[256,1024]{1,0:T(8,128)} %fusion.12.q_ref, f32[256,256]{1,0:T(8,128)} %fusion.10.kv_ref, f32[128,128]{1,0:T(8,128)} %get-tuple-element.51.cos_ref, f32[128,128]{1,0:T(8,128)} %get-tuple-element.52.sin_ref), custom_call_target="tpu_custom_call" | custom-call | flops 134217728 | bytes 1572864 | tf_op jit(solution)/shard_map/pallas_call | solution.py:60
  348.4 12.6 %fusion.8.q_ref = f32[256,1024]{1,0:T(8,128)} fusion(bf16[8192,1024]{1,0:T(8,128)(2,1)} %copy-done.2, bf16[256,8192]{1,0:T(8,128)(2,1)} %copy-done.3, f32[256]{0:T(256)S(1)} %add_rsqrt_fusion, f32[8192]{0:T(1024)S(1)} %copy-done.22), kind=kOutput, calls=%fused_computation.25 | convolution fusion | flops 4303355904 | bytes 22053888 | tf_op jit(solution)/shard_map/dot_general | solution.py:230
  360.9 3.2 constant_dynamic-update-slice_fusion.1
  364.2 10.5 %convolution_convert_fusion.1 = bf16[256,8192]{1,0:T(8,128)(2,1)S(1)} fusion(bf16[256,1024]{1,0:T(8,128)(2,1)S(1)} %copy-done.19, bf16[1024,8192]{1,0:T(8,128)(2,1)} %constant_dynamic-update-slice_fusion.1), kind=kOutput, calls=%fused_computation.6 | convolution fusion | flops 4297064448 | bytes 21495808 | tf_op jit(solution)/shard_map/dot_general | solution.py:233
  374.7 2.0 copy-done.6
  378.1 5.6 collective-permute-start.24
  383.7 7.5 %shard_map.96 = bf16[256,1024]{1,0:T(8,128)(2,1)} custom-call(f32[256,1024]{1,0:T(8,128)} %fusion.8.q_ref, f32[256,256]{1,0:T(8,128)} %fusion.6.kv_ref, f32[128,128]{1,0:T(8,128)} %get-tuple-element.51.cos_ref, f32[128,128]{1,0:T(8,128)} %get-tuple-element.52.sin_ref), custom_call_target="tpu_custom_call" | custom-call | flops 134217728 | bytes 1572864 | tf_op jit(solution)/shard_map/pallas_call | solution.py:60
  391.2 10.5 %convolution_convert_fusion = bf16[256,8192]{1,0:T(8,128)(2,1)S(1)} fusion(bf16[256,1024]{1,0:T(8,128)(2,1)} %shard_map.96, bf16[1024,8192]{1,0:T(8,128)(2,1)} %constant_dynamic-update-slice_fusion.1), kind=kOutput, calls=%fused_computation.5 | convolution fusion | flops 4297064448 | bytes 21495808 | tf_op jit(solution)/shard_map/dot_general | solution.py:233
  401.7 2.0 copy-done.4
  404.8 3.8 collective-permute-start.36
  411.4 2.9 add_convert_fusion.7
  414.4 6.1 %collective-permute-start.25 = (bf16[256,2048]{1,0:T(8,128)(2,1)}, bf16[256,2048]{1,0:T(8,128)(2,1)}, u32[]{:S(2)}, u32[]{:S(2)}) collective-permute-start(bf16[256,2048]{1,0:T(8,128)(2,1)} %add_convert_fusion.7), channel_id=1, source_target_pairs={{0,4},{4,8},{8,12},{1,5},{5,9},{9,13},{2,6},{6,10},{10,14},{3,7},{... | collective-permute-start | bytes 3145736 | tf_op jit(solution)/shard_map/ppermute | solution.py:148
  420.5 10.9 %collective-permute-done.36 = bf16[256,2048]{1,0:T(8,128)(2,1)} collective-permute-done((bf16[256,2048]{1,0:T(8,128)(2,1)}, bf16[256,2048]{1,0:T(8,128)(2,1)}, u32[]{:S(2)}, u32[]{:S(2)}) %collective-permute-start.36) | collective-permute-done | bytes 1048608 | tf_op jit(solution)/shard_map/ppermute | solution.py:148
  431.4 2.9 add_convert_fusion.3
  434.3 5.3 collective-permute-start.37
  439.8 14.0 %collective-permute-done.25 = bf16[256,2048]{1,0:T(8,128)(2,1)} collective-permute-done((bf16[256,2048]{1,0:T(8,128)(2,1)}, bf16[256,2048]{1,0:T(8,128)(2,1)}, u32[]{:S(2)}, u32[]{:S(2)}) %collective-permute-start.25) | collective-permute-done | bytes 1048608 | tf_op jit(solution)/shard_map/ppermute | solution.py:148
  453.9 4.5 add_convert_fusion.6
  459.6 16.0 %collective-permute-done.37 = bf16[256,2048]{1,0:T(8,128)(2,1)} collective-permute-done((bf16[256,2048]{1,0:T(8,128)(2,1)}, bf16[256,2048]{1,0:T(8,128)(2,1)}, u32[]{:S(2)}, u32[]{:S(2)}) %collective-permute-start.37) | collective-permute-done | bytes 1048608 | tf_op jit(solution)/shard_map/ppermute | solution.py:148
  475.6 3.3 add_convert_fusion.2
  480.2 6.0 %collective-permute-start.26 = (bf16[256,2048]{1,0:T(8,128)(2,1)}, bf16[256,2048]{1,0:T(8,128)(2,1)}, u32[]{:S(2)}, u32[]{:S(2)}) collective-permute-start(bf16[256,2048]{1,0:T(8,128)(2,1)} %get-tuple-element.6), channel_id=1, source_target_pairs={{0,4},{4,8},{8,12},{1,5},{5,9},{9,13},{2,6},{6,10},{10,14},{3,7},{... | collective-permute-start | bytes 3145736 | tf_op jit(solution)/shard_map/ppermute | solution.py:148
  486.2 3.9 collective-permute-start.38
  490.2 2.9 add_convert_fusion.4
  494.4 14.3 %collective-permute-done.40 = bf16[256,2048]{1,0:T(8,128)(2,1)} collective-permute-done((bf16[256,2048]{1,0:T(8,128)(2,1)S(1)}, bf16[256,2048]{1,0:T(8,128)(2,1)}, u32[]{:S(2)}, u32[]{:S(2)}) %collective-permute-start.40) | collective-permute-done | bytes 1048608 | tf_op jit(solution)/shard_map/ppermute | solution.py:149
  508.7 1.9 add_convert_fusion
  512.3 18.8 %collective-permute-done.29 = bf16[256,2048]{1,0:T(8,128)(2,1)} collective-permute-done((bf16[256,2048]{1,0:T(8,128)(2,1)}, bf16[256,2048]{1,0:T(8,128)(2,1)}, u32[]{:S(2)}, u32[]{:S(2)}) %collective-permute-start.29) | collective-permute-done | bytes 1048608 | tf_op jit(solution)/shard_map/ppermute | solution.py:149
  531.2 2.7 multiply_convert_fusion.1
  533.9 18.4 %collective-permute-done.41 = bf16[256,2048]{1,0:T(8,128)(2,1)} collective-permute-done((bf16[256,2048]{1,0:T(8,128)(2,1)S(1)}, bf16[256,2048]{1,0:T(8,128)(2,1)}, u32[]{:S(2)}, u32[]{:S(2)}) %collective-permute-start.41) | collective-permute-done | bytes 1048608 | tf_op jit(solution)/shard_map/ppermute | solution.py:149
  552.3 2.7 multiply_convert_fusion
  556.2 10.1 %all-reduce = (f32[8,3]{0,1:T(4,128)S(1)}, f32[8,1]{0,1:T(1,128)S(1)}) all-reduce(f32[8,3]{0,1:T(4,128)S(1)} %fusion.15, f32[8,1]{0,1:T(1,128)S(1)} %bitcast.62), channel_id=1, replica_groups=mesh['groups'=2,'tensor'=4,'dp'=4] {'tensor'}, use_global_device_ids=true, to_apply=%region_8.9 | all-reduce | flops 32 | bytes 256 | tf_op jit(solution)/shard_map/psum | solution.py:249
  566.4 6.1 %all_to_all.5 = f32[4,2,3]{2,1,0:T(2,128)S(1)} all-to-all(f32[4,2,3]{2,1,0:T(2,128)S(1)} %fusion.16), channel_id=1, replica_groups=mesh['groups'=2,'tensor'=4,'dp'=4] {'dp'}, dimensions={0} | all-to-all | bytes 192 | tf_op jit(solution)/shard_map/all_to_all | solution.py:254
  (182 shorter events, 66.8 us)
Async XLA Ops:
  0.6 555.4 %copy-start = (bf16[3,2048]{1,0:T(4,128)(2,1)S(1)}, bf16[3,2048]{1,0:T(4,128)(2,1)}, u32[]{:S(2)}) copy-start(bf16[3,2048]{1,0:T(4,128)(2,1)} %param.15) | copy-start | bytes 36868
  19.3 14.1 %collective-permute-start = (bf16[2,64,2048]{2,1,0:T(8,128)(2,1)S(1)}, bf16[2,64,2048]{2,1,0:T(8,128)(2,1)}, u32[]{:S(2)}, u32[]{:S(2)}) collective-permute-start(bf16[2,64,2048]{2,1,0:T(8,128)(2,1)S(1)} %pad_maximum_fusion.1), channel_id=1, source_target_pairs={{0,1},{1,2},{2,3},{3,0},{4,5},{5,6},{6,7},{7,4},{8,9},{9,10},{10,1... | collective-permute-start | bytes 1572872 | tf_op jit(solution)/shard_map/ppermute | solution.py:191
  19.9 15.4 %collective-permute-start.1 = (bf16[2,64,2048]{2,1,0:T(8,128)(2,1)S(1)}, bf16[2,64,2048]{2,1,0:T(8,128)(2,1)S(1)}, u32[]{:S(2)}, u32[]{:S(2)}) collective-permute-start(bf16[2,64,2048]{2,1,0:T(8,128)(2,1)S(1)} %pad_maximum_fusion.2), channel_id=1, source_target_pairs={{0,2},{1,3},{2,0},{3,1},{4,6},{5,7},{6,4},{7,5},{8,10},{9,11},{10,... | collective-permute-start | bytes 1572872 | tf_op jit(solution)/shard_map/ppermute | solution.py:191
  22.5 22.8 %collective-permute-start.2 = (bf16[2,64,2048]{2,1,0:T(8,128)(2,1)S(1)}, bf16[2,64,2048]{2,1,0:T(8,128)(2,1)S(1)}, u32[]{:S(2)}, u32[]{:S(2)}) collective-permute-start(bf16[2,64,2048]{2,1,0:T(8,128)(2,1)S(1)} %pad_maximum_fusion.3), channel_id=1, source_target_pairs={{0,3},{1,0},{2,1},{3,2},{4,7},{5,4},{6,5},{7,6},{8,11},{9,8},{10,9... | collective-permute-start | bytes 1572872 | tf_op jit(solution)/shard_map/ppermute | solution.py:191
  47.8 28.0 %collective-permute-start.4 = (bf16[256,2048]{1,0:T(8,128)(2,1)S(1)}, bf16[256,2048]{1,0:T(8,128)(2,1)}, u32[]{:S(2)}, u32[]{:S(2)}) collective-permute-start(bf16[256,2048]{1,0:T(8,128)(2,1)S(1)} %bitcast.57), channel_id=1, source_target_pairs={{4,0},{8,4},{12,8},{5,1},{9,5},{13,9},{6,2},{10,6},{14,10},{7,3},{... | collective-permute-start | bytes 3145736 | tf_op jit(solution)/shard_map/ppermute | solution.py:123
  54.1 23.4 %collective-permute-start.14 = (bf16[2048,256]{1,0:T(8,128)(2,1)}, bf16[2048,256]{1,0:T(8,128)(2,1)S(1)}, u32[]{:S(2)}, u32[]{:S(2)}) collective-permute-start(bf16[2048,256]{1,0:T(8,128)(2,1)} %get-tuple-element.5), channel_id=1, source_target_pairs={{0,1},{1,0},{2,3},{3,2},{4,5},{5,4},{6,7},{7,6},{8,9},{9,8},{10,11... | collective-permute-start | bytes 3145736 | tf_op jit(solution)/shard_map/ppermute | solution.py:107
  55.5 14.3 %collective-permute-start.15 = (bf16[1024,256]{1,0:T(8,128)(2,1)S(1)}, bf16[1024,256]{1,0:T(8,128)(2,1)S(1)}, u32[]{:S(2)}, u32[]{:S(2)}) collective-permute-start(bf16[1024,256]{1,0:T(8,128)(2,1)S(1)} %dynamic-slice_bitcast_fusion.1), channel_id=1, source_target_pairs={{0,2},{1,3},{2,0},{3,1},{4,6},{5,7},{6,4},{7,5},{8,10},{9,11},{10,... | collective-permute-start | bytes 1572872 | tf_op jit(solution)/shard_map/ppermute | solution.py:98
  57.7 3.7 copy-start.7
  57.7 40.6 %collective-permute-start.31 = (bf16[256,2048]{1,0:T(8,128)(2,1)S(1)}, bf16[256,2048]{1,0:T(8,128)(2,1)}, u32[]{:S(2)}, u32[]{:S(2)}) collective-permute-start(bf16[256,2048]{1,0:T(8,128)(2,1)S(1)} %bitcast.54), channel_id=1, source_target_pairs={{4,0},{8,4},{12,8},{5,1},{9,5},{13,9},{6,2},{10,6},{14,10},{7,3},{... | collective-permute-start | bytes 3145736 | tf_op jit(solution)/shard_map/ppermute | solution.py:123
  62.0 45.1 %copy-start.1 = (bf16[8192,1024]{1,0:T(8,128)(2,1)}, bf16[8192,1024]{1,0:T(8,128)(2,1)S(1)}, u32[]{:S(2)}) copy-start(bf16[8192,1024]{1,0:T(8,128)(2,1)S(1)} %constant_dynamic-update-slice_fusion.18) | copy-start | bytes 50331652
  62.0 37.6 %copy-start.9 = (bf16[1024,2048]{1,0:T(8,128)(2,1)S(1)}, bf16[1024,2048]{1,0:T(8,128)(2,1)}, u32[]{:S(2)}) copy-start(bf16[1024,2048]{1,0:T(8,128)(2,1)} %param.14) | copy-start | bytes 12582916
  69.8 37.3 %copy-start.15 = (bf16[1024,256]{1,0:T(8,128)(2,1)}, bf16[1024,256]{1,0:T(8,128)(2,1)S(1)}, u32[]{:S(2)}) copy-start(bf16[1024,256]{1,0:T(8,128)(2,1)S(1)} %collective-permute-done.15) | copy-start | bytes 1572868
  69.8 10.7 %collective-permute-start.16 = (bf16[1024,256]{1,0:T(8,128)(2,1)S(1)}, bf16[1024,256]{1,0:T(8,128)(2,1)S(1)}, u32[]{:S(2)}, u32[]{:S(2)}) collective-permute-start(bf16[1024,256]{1,0:T(8,128)(2,1)S(1)} %collective-permute-done.15), channel_id=1, source_target_pairs={{0,1},{1,0},{2,3},{3,2},{4,5},{5,4},{6,7},{7,6},{8,9},{9,8},{10,11... | collective-permute-start | bytes 1572872 | tf_op jit(solution)/shard_map/ppermute | solution.py:111
  69.8 40.2 %collective-permute-start.3 = (bf16[256,2048]{1,0:T(8,128)(2,1)S(1)}, bf16[256,2048]{1,0:T(8,128)(2,1)}, u32[]{:S(2)}, u32[]{:S(2)}) collective-permute-start(bf16[256,2048]{1,0:T(8,128)(2,1)S(1)} %bitcast.58), channel_id=1, source_target_pairs={{0,4},{4,8},{8,12},{1,5},{5,9},{9,13},{2,6},{6,10},{10,14},{3,7},{... | collective-permute-start | bytes 3145736 | tf_op jit(solution)/shard_map/ppermute | solution.py:122
  75.8 44.9 %collective-permute-start.5 = (bf16[256,2048]{1,0:T(8,128)(2,1)}, bf16[256,2048]{1,0:T(8,128)(2,1)}, u32[]{:S(2)}, u32[]{:S(2)}) collective-permute-start(bf16[256,2048]{1,0:T(8,128)(2,1)} %collective-permute-done.4), channel_id=1, source_target_pairs={{4,0},{8,4},{12,8},{5,1},{9,5},{13,9},{6,2},{10,6},{14,10},{7,3},{... | collective-permute-start | bytes 3145736 | tf_op jit(solution)/shard_map/ppermute | solution.py:123
  77.5 31.8 %collective-permute-start.17 = (bf16[1024,256]{1,0:T(8,128)(2,1)S(1)}, bf16[1024,256]{1,0:T(8,128)(2,1)}, u32[]{:S(2)}, u32[]{:S(2)}) collective-permute-start(bf16[1024,256]{1,0:T(8,128)(2,1)S(1)} %collective-permute-done.15), channel_id=1, source_target_pairs={{0,16},{16,0},{1,17},{17,1},{2,18},{18,2},{3,19},{19,3},{4,20},{20... | collective-permute-start | bytes 1572872 | tf_op jit(solution)/shard_map/ppermute | solution.py:102
  80.5 26.5 %copy-start.17 = (bf16[1024,256]{1,0:T(8,128)(2,1)}, bf16[1024,256]{1,0:T(8,128)(2,1)S(1)}, u32[]{:S(2)}) copy-start(bf16[1024,256]{1,0:T(8,128)(2,1)S(1)} %collective-permute-done.16) | copy-start | bytes 1572868
  80.5 42.8 %collective-permute-start.30 = (bf16[256,2048]{1,0:T(8,128)(2,1)S(1)}, bf16[256,2048]{1,0:T(8,128)(2,1)}, u32[]{:S(2)}, u32[]{:S(2)}) collective-permute-start(bf16[256,2048]{1,0:T(8,128)(2,1)S(1)} %bitcast.55), channel_id=1, source_target_pairs={{0,4},{4,8},{8,12},{1,5},{5,9},{9,13},{2,6},{6,10},{10,14},{3,7},{... | collective-permute-start | bytes 3145736 | tf_op jit(solution)/shard_map/ppermute | solution.py:122
  98.3 44.9 %collective-permute-start.32 = (bf16[256,2048]{1,0:T(8,128)(2,1)}, bf16[256,2048]{1,0:T(8,128)(2,1)}, u32[]{:S(2)}, u32[]{:S(2)}) collective-permute-start(bf16[256,2048]{1,0:T(8,128)(2,1)} %collective-permute-done.31), channel_id=1, source_target_pairs={{4,0},{8,4},{12,8},{5,1},{9,5},{13,9},{6,2},{10,6},{14,10},{7,3},{... | collective-permute-start | bytes 3145736 | tf_op jit(solution)/shard_map/ppermute | solution.py:123
  109.3 14.8 %collective-permute-start.18 = (bf16[1024,256]{1,0:T(8,128)(2,1)}, bf16[1024,256]{1,0:T(8,128)(2,1)}, u32[]{:S(2)}, u32[]{:S(2)}) collective-permute-start(bf16[1024,256]{1,0:T(8,128)(2,1)} %collective-permute-done.17), channel_id=1, source_target_pairs={{0,1},{1,0},{2,3},{3,2},{4,5},{5,4},{6,7},{7,6},{8,9},{9,8},{10,11... | collective-permute-start | bytes 1572872 | tf_op jit(solution)/shard_map/ppermute | solution.py:111
  110.1 40.9 %collective-permute-start.7 = (bf16[256,2048]{1,0:T(8,128)(2,1)}, bf16[256,2048]{1,0:T(8,128)(2,1)S(1)}, u32[]{:S(2)}, u32[]{:S(2)}) collective-permute-start(bf16[256,2048]{1,0:T(8,128)(2,1)} %collective-permute-done.3), channel_id=1, source_target_pairs={{0,4},{4,8},{8,12},{1,5},{5,9},{9,13},{2,6},{6,10},{10,14},{3,7},{... | collective-permute-start | bytes 3145736 | tf_op jit(solution)/shard_map/ppermute | solution.py:122
  120.8 44.8 %collective-permute-start.6 = (bf16[256,2048]{1,0:T(8,128)(2,1)}, bf16[256,2048]{1,0:T(8,128)(2,1)S(1)}, u32[]{:S(2)}, u32[]{:S(2)}) collective-permute-start(bf16[256,2048]{1,0:T(8,128)(2,1)} %collective-permute-done.5), channel_id=1, source_target_pairs={{4,0},{8,4},{12,8},{5,1},{9,5},{13,9},{6,2},{10,6},{14,10},{7,3},{... | collective-permute-start | bytes 3145736 | tf_op jit(solution)/shard_map/ppermute | solution.py:123
  122.7 22.9 %copy-start.16 = (bf16[1024,256]{1,0:T(8,128)(2,1)S(1)}, bf16[1024,256]{1,0:T(8,128)(2,1)}, u32[]{:S(2)}) copy-start(bf16[1024,256]{1,0:T(8,128)(2,1)} %copy-done.15) | copy-start | bytes 1572868
  122.7 23.7 %copy-start.18 = (bf16[1024,256]{1,0:T(8,128)(2,1)S(1)}, bf16[1024,256]{1,0:T(8,128)(2,1)}, u32[]{:S(2)}) copy-start(bf16[1024,256]{1,0:T(8,128)(2,1)} %copy-done.17) | copy-start | bytes 1572868
  123.2 27.8 %copy-start.8 = (bf16[2048,1024]{1,0:T(8,128)(2,1)S(1)}, bf16[2048,1024]{1,0:T(8,128)(2,1)}, u32[]{:S(2)}) copy-start(bf16[2048,1024]{1,0:T(8,128)(2,1)} %param.12) | copy-start | bytes 12582916
  123.2 42.4 %copy-start.14 = (bf16[1024,1024]{1,0:T(8,128)(2,1)S(1)}, bf16[1024,1024]{1,0:T(8,128)(2,1)}, u32[]{:S(2)}) copy-start(bf16[1024,1024]{1,0:T(8,128)(2,1)} %constant_dynamic-slice_fusion.4) | copy-start | bytes 6291460
  124.1 69.7 %collective-permute-start.10 = (bf16[1024,1024]{1,0:T(8,128)(2,1)S(1)}, bf16[1024,1024]{1,0:T(8,128)(2,1)}, u32[]{:S(2)}, u32[]{:S(2)}) collective-permute-start(bf16[1024,1024]{1,0:T(8,128)(2,1)S(1)} %copy-done.13), channel_id=1, source_target_pairs={{0,2},{1,3},{2,0},{3,1},{4,6},{5,7},{6,4},{7,5},{8,10},{9,11},{10,... | collective-permute-start | bytes 6291464 | tf_op jit(solution)/shard_map/ppermute | solution.py:98
  124.1 41.9 %collective-permute-start.34 = (bf16[256,2048]{1,0:T(8,128)(2,1)}, bf16[256,2048]{1,0:T(8,128)(2,1)S(1)}, u32[]{:S(2)}, u32[]{:S(2)}) collective-permute-start(bf16[256,2048]{1,0:T(8,128)(2,1)} %collective-permute-done.30), channel_id=1, source_target_pairs={{0,4},{4,8},{8,12},{1,5},{5,9},{9,13},{2,6},{6,10},{10,14},{3,7},{... | collective-permute-start | bytes 3145736 | tf_op jit(solution)/shard_map/ppermute | solution.py:122
  143.2 44.7 %collective-permute-start.33 = (bf16[256,2048]{1,0:T(8,128)(2,1)}, bf16[256,2048]{1,0:T(8,128)(2,1)S(1)}, u32[]{:S(2)}, u32[]{:S(2)}) collective-permute-start(bf16[256,2048]{1,0:T(8,128)(2,1)} %collective-permute-done.32), channel_id=1, source_target_pairs={{4,0},{8,4},{12,8},{5,1},{9,5},{13,9},{6,2},{10,6},{14,10},{7,3},{... | collective-permute-start | bytes 3145736 | tf_op jit(solution)/shard_map/ppermute | solution.py:123
  151.0 42.8 %copy-start.10 = (bf16[1024,2048]{1,0:T(8,128)(2,1)S(1)}, bf16[1024,2048]{1,0:T(8,128)(2,1)}, u32[]{:S(2)}) copy-start(bf16[1024,2048]{1,0:T(8,128)(2,1)} %param.14) | copy-start | bytes 12582916
  151.0 77.1 %collective-permute-start.9 = (bf16[2048,1024]{1,0:T(8,128)(2,1)S(1)}, bf16[2048,1024]{1,0:T(8,128)(2,1)S(1)}, u32[]{:S(2)}, u32[]{:S(2)}) collective-permute-start(bf16[2048,1024]{1,0:T(8,128)(2,1)S(1)} %copy-done.8), channel_id=1, source_target_pairs={{0,1},{1,0},{2,3},{3,2},{4,5},{5,4},{6,7},{7,6},{8,9},{9,8},{10,11... | collective-permute-start | bytes 12582920 | tf_op jit(solution)/shard_map/ppermute | solution.py:107
  165.6 51.0 %collective-permute-start.20 = (bf16[1024,1024]{1,0:T(8,128)(2,1)S(1)}, bf16[1024,1024]{1,0:T(8,128)(2,1)}, u32[]{:S(2)}, u32[]{:S(2)}) collective-permute-start(bf16[1024,1024]{1,0:T(8,128)(2,1)S(1)} %copy-done.14), channel_id=1, source_target_pairs={{0,2},{1,3},{2,0},{3,1},{4,6},{5,7},{6,4},{7,5},{8,10},{9,11},{10,... | collective-permute-start | bytes 6291464 | tf_op jit(solution)/shard_map/ppermute | solution.py:98
  166.0 50.6 %collective-permute-start.35 = (bf16[256,2048]{1,0:T(8,128)(2,1)S(1)}, bf16[256,2048]{1,0:T(8,128)(2,1)S(1)}, u32[]{:S(2)}, u32[]{:S(2)}) collective-permute-start(bf16[256,2048]{1,0:T(8,128)(2,1)S(1)} %collective-permute-done.34), channel_id=1, source_target_pairs={{0,4},{4,8},{8,12},{1,5},{5,9},{9,13},{2,6},{6,10},{10,14},{3,7},{... | collective-permute-start | bytes 3145736 | tf_op jit(solution)/shard_map/ppermute | solution.py:122
  187.9 30.4 %collective-permute-start.8 = (bf16[256,2048]{1,0:T(8,128)(2,1)S(1)}, bf16[256,2048]{1,0:T(8,128)(2,1)S(1)}, u32[]{:S(2)}, u32[]{:S(2)}) collective-permute-start(bf16[256,2048]{1,0:T(8,128)(2,1)S(1)} %collective-permute-done.7), channel_id=1, source_target_pairs={{0,4},{4,8},{8,12},{1,5},{5,9},{9,13},{2,6},{6,10},{10,14},{3,7},{... | collective-permute-start | bytes 3145736 | tf_op jit(solution)/shard_map/ppermute | solution.py:122
  193.8 124.5 %collective-permute-start.19 = (bf16[1024,2048]{1,0:T(8,128)(2,1)S(1)}, bf16[1024,2048]{1,0:T(8,128)(2,1)}, u32[]{:S(2)}, u32[]{:S(2)}) collective-permute-start(bf16[1024,2048]{1,0:T(8,128)(2,1)S(1)} %copy-done.10), channel_id=1, source_target_pairs={{0,1},{1,0},{2,3},{3,2},{4,5},{5,4},{6,7},{7,6},{8,9},{9,8},{10,11... | collective-permute-start | bytes 12582920 | tf_op jit(solution)/shard_map/ppermute | solution.py:107
  216.6 98.0 %collective-permute-start.11 = (bf16[1024,1024]{1,0:T(8,128)(2,1)}, bf16[1024,1024]{1,0:T(8,128)(2,1)}, u32[]{:S(2)}, u32[]{:S(2)}) collective-permute-start(bf16[1024,1024]{1,0:T(8,128)(2,1)} %collective-permute-done.10), channel_id=1, source_target_pairs={{0,1},{1,0},{2,3},{3,2},{4,5},{5,4},{6,7},{7,6},{8,9},{9,8},{10,11... | collective-permute-start | bytes 6291464 | tf_op jit(solution)/shard_map/ppermute | solution.py:111
  216.6 48.7 %collective-permute-start.12 = (bf16[1024,1024]{1,0:T(8,128)(2,1)}, bf16[1024,1024]{1,0:T(8,128)(2,1)}, u32[]{:S(2)}, u32[]{:S(2)}) collective-permute-start(bf16[1024,1024]{1,0:T(8,128)(2,1)} %collective-permute-done.10), channel_id=1, source_target_pairs={{0,16},{16,0},{1,17},{17,1},{2,18},{18,2},{3,19},{19,3},{4,20},{20... | collective-permute-start | bytes 6291464 | tf_op jit(solution)/shard_map/ppermute | solution.py:102
  218.3 91.6 %collective-permute-start.22 = (bf16[1024,1024]{1,0:T(8,128)(2,1)}, bf16[1024,1024]{1,0:T(8,128)(2,1)}, u32[]{:S(2)}, u32[]{:S(2)}) collective-permute-start(bf16[1024,1024]{1,0:T(8,128)(2,1)} %collective-permute-done.20), channel_id=1, source_target_pairs={{0,16},{16,0},{1,17},{17,1},{2,18},{18,2},{3,19},{19,3},{4,20},{20... | collective-permute-start | bytes 6291464 | tf_op jit(solution)/shard_map/ppermute | solution.py:102
  221.1 44.3 %copy-start.3 = (bf16[256,8192]{1,0:T(8,128)(2,1)}, bf16[256,8192]{1,0:T(8,128)(2,1)S(1)}, u32[]{:S(2)}) copy-start(bf16[256,8192]{1,0:T(8,128)(2,1)S(1)} %get-tuple-element.49) | copy-start | bytes 12582916
  221.1 88.9 %slice-start = ((s8[16777216]{0:T(1024)(128)(4,1)}), s8[4194304]{0:T(1024)(128)(4,1)S(1)}, s32[]{:S(2)}) async-start(s8[16777216]{0:T(1024)(128)(4,1)} %bitcast.52), calls=%async_computation.1 | async-start | bytes 8388608
  223.0 87.0 %slice-start.1 = ((s8[16777216]{0:T(1024)(128)(4,1)}), s8[4194304]{0:T(1024)(128)(4,1)S(1)}, s32[]{:S(2)}) async-start(s8[16777216]{0:T(1024)(128)(4,1)} %bitcast.52), calls=%async_computation.2 | async-start | bytes 8388608
  223.0 87.0 %slice-start.2 = ((s8[16777216]{0:T(1024)(128)(4,1)}), s8[4194304]{0:T(1024)(128)(4,1)S(1)}, s32[]{:S(2)}) async-start(s8[16777216]{0:T(1024)(128)(4,1)} %bitcast.52), calls=%async_computation.3 | async-start | bytes 8388608
  230.1 96.1 %collective-permute-start.21 = (bf16[1024,1024]{1,0:T(8,128)(2,1)}, bf16[1024,1024]{1,0:T(8,128)(2,1)}, u32[]{:S(2)}, u32[]{:S(2)}) collective-permute-start(bf16[1024,1024]{1,0:T(8,128)(2,1)} %collective-permute-done.20), channel_id=1, source_target_pairs={{0,1},{1,0},{2,3},{3,2},{4,5},{5,4},{6,7},{7,6},{8,9},{9,8},{10,11... | collective-permute-start | bytes 6291464 | tf_op jit(solution)/shard_map/ppermute | solution.py:111
  230.1 79.8 %slice-start.3 = ((s8[16777216]{0:T(1024)(128)(4,1)}), s8[4194304]{0:T(1024)(128)(4,1)S(1)}, s32[]{:S(2)}) async-start(s8[16777216]{0:T(1024)(128)(4,1)} %bitcast.52), calls=%async_computation.4 | async-start | bytes 8388608
  265.4 67.1 %collective-permute-start.13 = (bf16[1024,1024]{1,0:T(8,128)(2,1)}, bf16[1024,1024]{1,0:T(8,128)(2,1)}, u32[]{:S(2)}, u32[]{:S(2)}) collective-permute-start(bf16[1024,1024]{1,0:T(8,128)(2,1)} %collective-permute-done.12), channel_id=1, source_target_pairs={{0,1},{1,0},{2,3},{3,2},{4,5},{5,4},{6,7},{7,6},{8,9},{9,8},{10,11... | collective-permute-start | bytes 6291464 | tf_op jit(solution)/shard_map/ppermute | solution.py:111
  309.9 51.0 %collective-permute-start.23 = (bf16[1024,1024]{1,0:T(8,128)(2,1)}, bf16[1024,1024]{1,0:T(8,128)(2,1)}, u32[]{:S(2)}, u32[]{:S(2)}) collective-permute-start(bf16[1024,1024]{1,0:T(8,128)(2,1)} %collective-permute-done.22), channel_id=1, source_target_pairs={{0,1},{1,0},{2,3},{3,2},{4,5},{5,4},{6,7},{7,6},{8,9},{9,8},{10,11... | collective-permute-start | bytes 6291464 | tf_op jit(solution)/shard_map/ppermute | solution.py:111
  334.4 6.5 %copy-start.2 = (bf16[8192,1024]{1,0:T(8,128)(2,1)}, bf16[8192,1024]{1,0:T(8,128)(2,1)S(1)}, u32[]{:S(2)}) copy-start(bf16[8192,1024]{1,0:T(8,128)(2,1)S(1)} %constant_dynamic-update-slice_fusion.13) | copy-start | bytes 50331652
  360.9 3.2 copy-start.19
  378.1 33.3 %collective-permute-start.24 = (bf16[256,2048]{1,0:T(8,128)(2,1)}, bf16[256,2048]{1,0:T(8,128)(2,1)}, u32[]{:S(2)}, u32[]{:S(2)}) collective-permute-start(bf16[256,2048]{1,0:T(8,128)(2,1)} %get-tuple-element.8), channel_id=1, source_target_pairs={{0,4},{4,8},{8,12},{1,5},{5,9},{9,13},{2,6},{6,10},{10,14},{3,7},{... | collective-permute-start | bytes 3145736 | tf_op jit(solution)/shard_map/ppermute | solution.py:148
  403.7 4.9 copy-start.20
  404.8 34.8 %copy-start.21 = (s32[32]{0:T(128)S(1)}, s32[32]{0:T(128)}, u32[]{:S(2)}) copy-start(s32[32]{0:T(128)} %param.9) | copy-start | bytes 388
  404.8 26.6 %collective-permute-start.36 = (bf16[256,2048]{1,0:T(8,128)(2,1)}, bf16[256,2048]{1,0:T(8,128)(2,1)}, u32[]{:S(2)}, u32[]{:S(2)}) collective-permute-start(bf16[256,2048]{1,0:T(8,128)(2,1)} %get-tuple-element.12), channel_id=1, source_target_pairs={{0,4},{4,8},{8,12},{1,5},{5,9},{9,13},{2,6},{6,10},{10,14},{3,7},{... | collective-permute-start | bytes 3145736 | tf_op jit(solution)/shard_map/ppermute | solution.py:148
  408.8 31.0 %collective-permute-start.27 = (bf16[256,2048]{1,0:T(8,128)(2,1)}, bf16[256,2048]{1,0:T(8,128)(2,1)}, u32[]{:S(2)}, u32[]{:S(2)}) collective-permute-start(bf16[256,2048]{1,0:T(8,128)(2,1)} %get-tuple-element.9), channel_id=1, source_target_pairs={{4,0},{8,4},{12,8},{5,1},{9,5},{13,9},{6,2},{10,6},{14,10},{7,3},{... | collective-permute-start | bytes 3145736 | tf_op jit(solution)/shard_map/ppermute | solution.py:149
  410.1 49.5 %collective-permute-start.39 = (bf16[256,2048]{1,0:T(8,128)(2,1)S(1)}, bf16[256,2048]{1,0:T(8,128)(2,1)}, u32[]{:S(2)}, u32[]{:S(2)}) collective-permute-start(bf16[256,2048]{1,0:T(8,128)(2,1)S(1)} %get-tuple-element.13), channel_id=1, source_target_pairs={{4,0},{8,4},{12,8},{5,1},{9,5},{13,9},{6,2},{10,6},{14,10},{7,3},{... | collective-permute-start | bytes 3145736 | tf_op jit(solution)/shard_map/ppermute | solution.py:149
  414.4 39.5 %collective-permute-start.25 = (bf16[256,2048]{1,0:T(8,128)(2,1)}, bf16[256,2048]{1,0:T(8,128)(2,1)}, u32[]{:S(2)}, u32[]{:S(2)}) collective-permute-start(bf16[256,2048]{1,0:T(8,128)(2,1)} %add_convert_fusion.7), channel_id=1, source_target_pairs={{0,4},{4,8},{8,12},{1,5},{5,9},{9,13},{2,6},{6,10},{10,14},{3,7},{... | collective-permute-start | bytes 3145736 | tf_op jit(solution)/shard_map/ppermute | solution.py:148
  434.3 41.3 %collective-permute-start.37 = (bf16[256,2048]{1,0:T(8,128)(2,1)}, bf16[256,2048]{1,0:T(8,128)(2,1)}, u32[]{:S(2)}, u32[]{:S(2)}) collective-permute-start(bf16[256,2048]{1,0:T(8,128)(2,1)} %add_convert_fusion.3), channel_id=1, source_target_pairs={{0,4},{4,8},{8,12},{1,5},{5,9},{9,13},{2,6},{6,10},{10,14},{3,7},{... | collective-permute-start | bytes 3145736 | tf_op jit(solution)/shard_map/ppermute | solution.py:148
  439.8 35.8 %copy-start.5 = (bf16[256,8192]{1,0:T(8,128)(2,1)S(1)}, bf16[256,8192]{1,0:T(8,128)(2,1)}, u32[]{:S(2)}) copy-start(bf16[256,8192]{1,0:T(8,128)(2,1)} %copy-done.4) | copy-start | bytes 12582916
  458.3 31.8 %collective-permute-start.28 = (bf16[256,2048]{1,0:T(8,128)(2,1)}, bf16[256,2048]{1,0:T(8,128)(2,1)}, u32[]{:S(2)}, u32[]{:S(2)}) collective-permute-start(bf16[256,2048]{1,0:T(8,128)(2,1)} %get-tuple-element.7), channel_id=1, source_target_pairs={{4,0},{8,4},{12,8},{5,1},{9,5},{13,9},{6,2},{10,6},{14,10},{7,3},{... | collective-permute-start | bytes 3145736 | tf_op jit(solution)/shard_map/ppermute | solution.py:149
  478.9 29.8 %collective-permute-start.40 = (bf16[256,2048]{1,0:T(8,128)(2,1)S(1)}, bf16[256,2048]{1,0:T(8,128)(2,1)}, u32[]{:S(2)}, u32[]{:S(2)}) collective-permute-start(bf16[256,2048]{1,0:T(8,128)(2,1)S(1)} %get-tuple-element.11), channel_id=1, source_target_pairs={{4,0},{8,4},{12,8},{5,1},{9,5},{13,9},{6,2},{10,6},{14,10},{7,3},{... | collective-permute-start | bytes 3145736 | tf_op jit(solution)/shard_map/ppermute | solution.py:149
  480.2 32.1 %collective-permute-start.26 = (bf16[256,2048]{1,0:T(8,128)(2,1)}, bf16[256,2048]{1,0:T(8,128)(2,1)}, u32[]{:S(2)}, u32[]{:S(2)}) collective-permute-start(bf16[256,2048]{1,0:T(8,128)(2,1)} %get-tuple-element.6), channel_id=1, source_target_pairs={{0,4},{4,8},{8,12},{1,5},{5,9},{9,13},{2,6},{6,10},{10,14},{3,7},{... | collective-permute-start | bytes 3145736 | tf_op jit(solution)/shard_map/ppermute | solution.py:148
  486.2 47.7 %collective-permute-start.38 = (bf16[256,2048]{1,0:T(8,128)(2,1)}, bf16[256,2048]{1,0:T(8,128)(2,1)}, u32[]{:S(2)}, u32[]{:S(2)}) collective-permute-start(bf16[256,2048]{1,0:T(8,128)(2,1)} %get-tuple-element.10), channel_id=1, source_target_pairs={{0,4},{4,8},{8,12},{1,5},{5,9},{9,13},{2,6},{6,10},{10,14},{3,7},{... | collective-permute-start | bytes 3145736 | tf_op jit(solution)/shard_map/ppermute | solution.py:148
  493.1 38.1 %collective-permute-start.29 = (bf16[256,2048]{1,0:T(8,128)(2,1)}, bf16[256,2048]{1,0:T(8,128)(2,1)}, u32[]{:S(2)}, u32[]{:S(2)}) collective-permute-start(bf16[256,2048]{1,0:T(8,128)(2,1)} %add_convert_fusion.4), channel_id=1, source_target_pairs={{4,0},{8,4},{12,8},{5,1},{9,5},{13,9},{6,2},{10,6},{14,10},{7,3},{... | collective-permute-start | bytes 3145736 | tf_op jit(solution)/shard_map/ppermute | solution.py:149
  510.6 41.7 %collective-permute-start.41 = (bf16[256,2048]{1,0:T(8,128)(2,1)S(1)}, bf16[256,2048]{1,0:T(8,128)(2,1)}, u32[]{:S(2)}, u32[]{:S(2)}) collective-permute-start(bf16[256,2048]{1,0:T(8,128)(2,1)S(1)} %add_convert_fusion), channel_id=1, source_target_pairs={{4,0},{8,4},{12,8},{5,1},{9,5},{13,9},{6,2},{10,6},{14,10},{7,3},{... | collective-permute-start | bytes 3145736 | tf_op jit(solution)/shard_map/ppermute | solution.py:149
  555.2 18.1 %copy-start.12 = (bf16[512,2048]{1,0:T(8,128)(2,1)}, bf16[512,2048]{1,0:T(8,128)(2,1)S(1)}, u32[]{:S(2)}) copy-start(bf16[512,2048]{1,0:T(8,128)(2,1)S(1)} %pad_maximum_fusion) | copy-start | bytes 6291460
  (5 other events, 9.5 us)

commit v2 on v0

v2 whole, which is shorter than its diff:
```python
import functools
import math

import jax
import jax.numpy as jnp
from jax import lax
from jax.experimental import pallas as pl
from jax.experimental.pallas import tpu as pltpu
from jax.sharding import PartitionSpec as P

D = 8192
HD = 128
QH = 32
KVH = 4
OBJ = 3
CAP = 2
CHUNKS = 4
WPIECES = 4

EPS = 1e-05
THETA = 500000.0


def rotary_tables(row_count, period, head_size):
    positions = (jnp.arange(row_count, dtype=jnp.int32) % period).astype(jnp.float32)
    half_size = head_size // 2
    exponents = jnp.arange(half_size, dtype=jnp.float32) * (2.0 / head_size)
    inverse = jnp.power(jnp.float32(THETA), -exponents)
    angles = positions[:, None] * inverse[None, :]
    return (jnp.cos(angles), jnp.sin(angles))


MESH = pl.DeviceIdType.MESH


def kernel(dims, rows_ref, wq_hbm, kv_hbm, wo_hbm, gain_ref, cos_ref, sin_ref, out_hbm,
           wq, kv, wo, xg, up_slot, down_slot, queries, keyval, attended,
           own_sem, core_send, core_recv, x_send, x_recv, y_send, y_recv,
           own_core_send, own_core_recv,
           gather_send, gather_recv, sum_send, sum_recv, out_sem):
    n, groups, count, slot_len = dims
    chips = n // 2
    me, group, t = lax.axis_index("dp"), lax.axis_index("groups"), lax.axis_index("tensor")
    chunk_rows = xg.shape[2]
    chunks = xg.shape[0]
    width = xg.shape[3]
    heads = queries.shape[1] // HD
    mate = {"dp": me + 1 - 2 * lax.rem(me, 2)}
    above, below = {"tensor": t + 1}, {"tensor": t - 1}

    def remote(src, dst, send, recv, where):
        return pltpu.make_async_remote_copy(
            src_ref=src, dst_ref=dst, send_sem=send, recv_sem=recv,
            device_id=where, device_id_type=MESH)

    barrier = pltpu.get_barrier_semaphore()
    pl.semaphore_signal(barrier, inc=1, device_id=mate, device_id_type=MESH)
    for k in range(1, chips):
        pl.semaphore_signal(barrier, inc=1, device_id={"dp": lax.rem(me + 2 * k, n)}, device_id_type=MESH)
    for k in range(1, groups):
        pl.semaphore_signal(barrier, inc=1, device_id={"groups": lax.rem(group + k, groups)}, device_id_type=MESH)

    @pl.when(t < count - 1)
    def _():
        pl.semaphore_signal(barrier, inc=1, device_id=above, device_id_type=MESH)

    @pl.when(t > 0)
    def _():
        pl.semaphore_signal(barrier, inc=1, device_id=below, device_id_type=MESH)

    neighbours = jnp.where(t < count - 1, 1, 0) + jnp.where(t > 0, 1, 0)
    pl.semaphore_wait(barrier, 1 + (chips - 1) + (groups - 1) + neighbours)

    arrays = [(kv_hbm, kv, 1), (wq_hbm, wq, WPIECES), (wo_hbm, wo, WPIECES)]
    pieces = []
    for a, (shard, full, parts) in enumerate(arrays):
        size = shard.shape[0] // groups // parts
        for p in range(parts):
            pieces.append((a, shard, full, p, size))

    def place(i, device, which):
        a, shard, full, p, size = pieces[i]
        start = which * (shard.shape[0] // groups) + p * size
        return full.at[device, pl.ds(pl.multiple_of(start, size), size)]

    def x_copy(i, k):
        a, shard, full, p, size = pieces[i]
        start = group * (shard.shape[0] // groups) + p * size
        return remote(shard.at[pl.ds(pl.multiple_of(start, size), size)], place(i, me, group),
                      x_send.at[i, k - 1], x_recv.at[i, k - 1], {"dp": lax.rem(me + 2 * k, n)})

    def origin(k):
        return lax.rem(me - 2 * k + n, n)

    def y_copy(i, k, o):
        spot = place(i, origin(k), group)
        return remote(spot, spot, y_send.at[i, k - 1, o - 1], y_recv.at[i, k - 1, o - 1],
                      {"groups": lax.rem(group + o, groups)})

    def core_copy(i, k, o):
        spot = place(i, origin(k), lax.rem(group - o + groups, groups))
        return remote(spot, spot, core_send.at[i, k - 1, o], core_recv.at[i, k - 1, o], mate)

    def x_start(i):
        if i < len(pieces):
            for k in range(1, chips):
                x_copy(i, k).start()

    def x_event(i):
        for k in range(1, chips):
            x_copy(i, k).wait()
            for o in range(1, groups):
                y_copy(i, k, o).start()
            core_copy(i, k, 0).start()
        x_start(i + 2)

    def y_event(i):
        for k in range(1, chips):
            for o in range(1, groups):
                y_copy(i, k, o).wait()
                core_copy(i, k, o).start()

    def c_event(i):
        for k in range(1, chips):
            for o in range(groups):
                core_copy(i, k, o).wait()

    def own_copy(a):
        shard, full, _ = arrays[a]
        return pltpu.make_async_copy(shard, full.at[me], own_sem.at[a])

    def own_core(a):
        shard, full, _ = arrays[a]
        return remote(shard, full.at[me], own_core_send.at[a], own_core_recv.at[a], mate)

    def gather_copy(c, s, upward):
        d = 0 if upward else 1
        block = t - (s - 1) if upward else t + (s - 1)
        spot = xg.at[c, jnp.clip(block, 0, count - 1)]
        src = rows_ref.at[pl.ds(c * chunk_rows, chunk_rows)] if s == 1 else spot
        return remote(src, spot, gather_send.at[c, s - 1, d], gather_recv.at[c, s - 1, d],
                      above if upward else below)

    def gather_step(c, s):
        if c >= chunks:
            return
        for upward in (True, False):
            have = (t - (s - 1) >= 0) if upward else (t + (s - 1) <= count - 1)
            more = (t < count - 1) if upward else (t > 0)
            if s > 1:
                @pl.when(have)
                def _():
                    gather_copy(c, s - 1, upward).wait_recv()
            if s < count:
                @pl.when(have & more)
                def _():
                    gather_copy(c, s, upward).start()

    def gather_sent(c):
        for s in range(1, count):
            for upward in (True, False):
                have = (t - (s - 1) >= 0) if upward else (t + (s - 1) <= count - 1)
                more = (t < count - 1) if upward else (t > 0)

                @pl.when(have & more)
                def _():
                    gather_copy(c, s, upward).wait_send()

    def sum_copy(c, s, upward, edge):
        d = 0 if upward else 1
        slot = up_slot if upward else down_slot
        if edge:
            target = count - 1 - s if upward else s
            src = xg.at[c, target]
        else:
            src = slot.at[c, s - 1]
        return remote(src, slot.at[c, s], sum_send.at[c, s, d], sum_recv.at[c, s, d],
                      above if upward else below)

    def sum_step(c, s):
        for upward in (True, False):
            place_of = t if upward else count - 1 - t
            slot = up_slot if upward else down_slot

            @pl.when(place_of == 0)
            def _():
                sum_copy(c, s, upward, True).start()

            if s > 0:
                @pl.when((place_of > 0) & (place_of <= s))
                def _():
                    sum_copy(c, s - 1, upward, False if s > 1 else True).wait_recv()
                    target = count - 1 - s + t if upward else s - (count - 1 - t)
                    target = jnp.clip(target, 0, count - 1)

                    @pl.loop(0, chunk_rows // 16)
                    def _(r):
                        at = pl.ds(pl.multiple_of(r * 16, 16), 16)
                        slot[c, s - 1, at, :] = (
                            slot[c, s - 1, at, :].astype(jnp.float32)
                            + xg[c, target, at, :].astype(jnp.float32)
                        ).astype(jnp.bfloat16)

                    sum_copy(c, s, upward, False).start()

    def sum_end(c):
        last = count - 2

        @pl.when(t > 0)
        def _():
            sum_copy(c, last, True, True).wait_recv()

        @pl.when(t < count - 1)
        def _():
            sum_copy(c, last, False, True).wait_recv()

        def finish(terms):
            @pl.loop(0, chunk_rows // 16)
            def _(r):
                at = pl.ds(pl.multiple_of(r * 16, 16), 16)
                total = xg[c, t, at, :].astype(jnp.float32)
                for slot in terms:
                    total = total + slot[c, last, at, :].astype(jnp.float32)
                local = rows_ref[pl.ds(pl.multiple_of(c * chunk_rows + r * 16, 16), 16), :]
                xg[c, t, at, :] = (local.astype(jnp.float32) + total).astype(jnp.bfloat16)

        @pl.when(t == 0)
        def _():
            finish((down_slot,))

        @pl.when(t == count - 1)
        def _():
            finish((up_slot,))

        @pl.when((t > 0) & (t < count - 1))
        def _():
            finish((up_slot, down_slot))

        out_copy(c).start()

    def out_copy(c):
        return pltpu.make_async_copy(
            xg.at[c, t], out_hbm.at[pl.ds(c * chunk_rows, chunk_rows)], out_sem.at[c])

    def sum_sent(c):
        for s in range(count - 1):
            for upward in (True, False):
                place_of = t if upward else count - 1 - t

                @pl.when(place_of <= s)
                def _():
                    sum_copy(c, s, upward, True).wait_send()

    def norm(c):
        gather_sent(c)

        @pl.loop(0, chunk_rows // 16)
        def _(r):
            at = pl.ds(pl.multiple_of(r * 16, 16), 16)
            xg[c, t, at, :] = rows_ref[pl.ds(pl.multiple_of(c * chunk_rows + r * 16, 16), 16), :]
            total = jnp.zeros((16, 1), jnp.float32)
            for b in range(count):
                wide = xg[c, b, at, :].astype(jnp.float32)
                total = total + jnp.sum(wide * wide, axis=1, keepdims=True)
            scale = lax.rsqrt(total / (count * width) + EPS)
            for b in range(count):
                wide = xg[c, b, at, :].astype(jnp.float32)
                xg[c, b, at, :] = (wide * scale * gain_ref[:, b * width:(b + 1) * width]).astype(jnp.bfloat16)

    def project(c, full, target, tile):
        depth = full.shape[1]
        reach = min(depth, width)

        @pl.loop(0, target.shape[1] // tile)
        def _(i):
            cols = pl.ds(pl.multiple_of(i * tile, tile), tile)
            total = jnp.zeros((chunk_rows, tile), jnp.float32)
            for b in range(count * width // reach):
                d, inner = divmod(b * reach, depth)
                e, outer = divmod(b * reach, width)
                total = total + jnp.dot(
                    xg[c, e, :, outer:outer + reach],
                    full[d, inner:inner + reach, cols],
                    preferred_element_type=jnp.float32)
            target[:, cols] = total

    def attend():
        step = 2 * slot_len
        cosine, sine = cos_ref[...], sin_ref[...]

        def turn(x):
            return (x * cosine + pltpu.roll(x, HD // 2, 1) * sine).astype(jnp.bfloat16)

        row_ids = lax.broadcasted_iota(jnp.int32, (step, step), 0)
        key_ids = lax.broadcasted_iota(jnp.int32, (step, step), 1)
        first = row_ids < slot_len
        allowed = (row_ids >= key_ids) & ((key_ids >= slot_len) | first)
        for p in range(chunk_rows // step):
            at = slice(p * step, (p + 1) * step)
            key = turn(keyval[at, :HD])
            value = keyval[at, HD:].astype(jnp.bfloat16)
            for head in range(heads):
                here = slice(head * HD, (head + 1) * HD)
                scores = lax.dot_general(
                    turn(queries[at, here]), key, (((1,), (1,)), ((), ())),
                    preferred_element_type=jnp.float32) * (1.0 / math.sqrt(HD))
                scores = jnp.where(allowed, scores, -1e30)
                weights = jnp.exp(scores - jnp.max(scores, axis=1, keepdims=True))
                weights = (weights / jnp.sum(weights, axis=1, keepdims=True)).astype(jnp.bfloat16)
                attended[at, here] = jnp.dot(
                    weights, value, preferred_element_type=jnp.float32).astype(jnp.bfloat16)

    def output(c):
        span = wo.shape[2]
        tile = min(256, width)
        for j in range(count):
            d, base = divmod(j * width, span)

            @pl.loop(0, width // tile)
            def _(i):
                cols = pl.ds(pl.multiple_of(i * tile, tile), tile)
                wide = pl.ds(pl.multiple_of(base + i * tile, tile), tile)
                xg[c, j, :, cols] = jnp.dot(
                    attended[...], wo[d, :, wide],
                    preferred_element_type=jnp.float32).astype(jnp.bfloat16)

    total = len(pieces)
    early = 1 + WPIECES
    x_start(0)
    x_start(1)
    gather_step(0, 1)
    for a in range(3):
        own_core(a).start()
        own_copy(a).start()
    order = []
    for i in range(early):
        order.append((x_event, i))
        if i:
            order.append((y_event, i - 1))
    order.append((x_event, early))
    order.append((y_event, early - 1))
    steps = [(0, s) for s in range(2, count + 1)] + [(1, s) for s in range(1, count + 1)] + [(2, 1)]
    for i in range(max(len(order), len(steps))):
        if i < len(steps):
            gather_step(*steps[i])
        if i < len(order):
            order[i][0](order[i][1])
    for a in range(3):
        own_core(a).wait()
        own_copy(a).wait()
    for i in range(early):
        c_event(i)

    for c in range(chunks):
        if c == 0:
            x_event(early + 1)
            y_event(early)
        norm(c)
        project(c, kv, keyval, 256)
        if c:
            for s in range(1, count - 1):
                if s <= (count - 1) // 2:
                    sum_step(c - 1, s)
        project(c, wq, queries, 256)
        for s in range(2, count // 2 + 1):
            gather_step(c + 2, s)
        if c:
            for s in range(1, count - 1):
                if s > (count - 1) // 2:
                    sum_step(c - 1, s)
        attend()
        for s in range(count // 2 + 1, count):
            gather_step(c + 2, s)
        if c == 0:
            for i in range(early + 1, total):
                if i + 1 < total:
                    x_event(i + 1)
                y_event(i)
            for i in range(early, total):
                c_event(i)
        output(c)
        sum_step(c, 0)
        if c:
            sum_end(c - 1)
        gather_step(c + 2, count)
        gather_step(c + 3, 1)
    for s in range(1, count - 1):
        sum_step(chunks - 1, s)
    sum_end(chunks - 1)
    for c in range(chunks):
        sum_sent(c)
        out_copy(c).wait()


def layer(local, w_query, kv_shard, w_out, ln_gain, cosine, sine, slot_len):
    n, groups, count = lax.axis_size("dp"), lax.axis_size("groups"), lax.axis_size("tensor")
    rows, width = local.shape
    chunk_rows = rows // CHUNKS
    pieces = 1 + 2 * WPIECES
    dma = pltpu.SemaphoreType.DMA
    chips = n // 2
    hops = max(1, chips - 1)
    others = max(1, groups - 1)
    whole = pl.BlockSpec(memory_space=pltpu.VMEM)
    remain = pl.BlockSpec(memory_space=pl.ANY)
    heads_width = w_query.shape[1]
    bf16 = jnp.bfloat16
    return pl.pallas_call(
        functools.partial(kernel, (n, groups, count, slot_len)),
        out_shape=jax.ShapeDtypeStruct((rows, width), bf16),
        in_specs=[whole, remain, remain, remain, whole, whole, whole],
        out_specs=remain,
        scratch_shapes=[
            pltpu.VMEM((n,) + w_query.shape, bf16),
            pltpu.VMEM((n,) + kv_shard.shape, bf16),
            pltpu.VMEM((n,) + w_out.shape, bf16),
            pltpu.VMEM((CHUNKS, count, chunk_rows, width), bf16),
            pltpu.VMEM((CHUNKS, count - 1, chunk_rows, width), bf16),
            pltpu.VMEM((CHUNKS, count - 1, chunk_rows, width), bf16),
            pltpu.VMEM((chunk_rows, heads_width), jnp.float32),
            pltpu.VMEM((chunk_rows, 2 * HD), jnp.float32),
            pltpu.VMEM((chunk_rows, heads_width), bf16),
            dma((3,)),
            dma((pieces, hops, groups)), dma((pieces, hops, groups)),
            dma((pieces, hops)), dma((pieces, hops)),
            dma((pieces, hops, others)), dma((pieces, hops, others)),
            dma((3,)), dma((3,)),
            dma((CHUNKS, count, 2)), dma((CHUNKS, count, 2)),
            dma((CHUNKS, count, 2)), dma((CHUNKS, count, 2)),
            dma((CHUNKS,)),
        ],
        compiler_params=pltpu.CompilerParams(
            collective_id=0, has_side_effects=True, vmem_limit_bytes=63 * 1024 * 1024),
        cost_estimate=pl.CostEstimate(
            flops=rows * D * heads_width * 5, bytes_accessed=60 * 2**20, transcendentals=rows * 2**10),
    )(local, w_query, kv_shard, w_out, ln_gain.reshape(1, -1), cosine, sine)


def body(gen_states, lengths, route, ln_gain, w_query, w_keyval, w_out, w_score):
    n = lax.axis_size("dp")
    me = lax.axis_index("dp")
    tensor_count = lax.axis_size("tensor")
    tensor_index = lax.axis_index("tensor")
    resp_dev, slot_len, width_part = gen_states.shape
    heads_here = w_query.shape[1] // HD
    row_count = resp_dev * slot_len
    route_table = route.reshape(n, resp_dev)
    my_routes = lax.dynamic_index_in_dim(route_table, me, 0, keepdims=False)
    slot_ids = jnp.arange(resp_dev, dtype=jnp.int32)
    earlier = slot_ids[None, :] < slot_ids[:, None]
    same_target = my_routes[:, None] == my_routes[None, :]
    sender_ranks = jnp.sum((earlier & same_target).astype(jnp.int32), axis=1)
    device_ids = jnp.arange(n, dtype=jnp.int32)
    capacity_ids = jnp.arange(CAP, dtype=jnp.int32)
    select = (my_routes[None, None, :] == device_ids[:, None, None]) & (
        sender_ranks[None, None, :] == capacity_ids[None, :, None]
    )
    picks = jnp.sum(jnp.where(select, slot_ids[None, None, :], 0), axis=2)
    arrivals = route_table == me
    counts = jnp.sum(arrivals.astype(jnp.int32), axis=1)
    offsets = jnp.cumsum(counts) - counts
    states = jnp.zeros((resp_dev + CAP, slot_len, width_part), gen_states.dtype)
    for shift in range(n):
        target = (me + shift) % n
        pair = jnp.concatenate(
            [
                lax.dynamic_slice_in_dim(gen_states, picks[target, j], 1, 0)
                for j in range(CAP)
            ],
            axis=0,
        )
        if shift:
            pair = lax.ppermute(pair, "dp", [(i, (i + shift) % n) for i in range(n)])
        source = (me - shift + n) % n
        start = jnp.where(counts[source] > 0, offsets[source], resp_dev)
        states = lax.dynamic_update_slice_in_dim(states, pair, start, 0)

    reward_ids = slot_ids
    placing = (
        reward_ids[:, None, None] == offsets[None, :, None] + capacity_ids[None, None, :]
    ) & (capacity_ids[None, None, :] < counts[None, :, None])
    placing = placing.reshape(resp_dev, n * CAP)
    flat_arrivals = arrivals.reshape(-1).astype(jnp.int32)
    places = jnp.cumsum(flat_arrivals) - 1
    owners = (places[None, :] == reward_ids[:, None]) & (flat_arrivals[None, :] == 1)
    reward_lengths = jnp.sum(jnp.where(owners, lengths[None, :], 0), axis=1)

    kv_index = tensor_index * heads_here // (QH // KVH)
    kv_shard = lax.dynamic_index_in_dim(w_keyval, kv_index, 0, keepdims=False)
    cosine, sine = rotary_tables(2 * slot_len, slot_len, HD)
    cosine = jnp.concatenate([cosine, cosine], axis=1)
    sine = jnp.concatenate([-sine, sine], axis=1)

    local = states[:resp_dev].reshape(row_count, width_part)
    summed = layer(local, w_query, kv_shard, w_out, ln_gain, cosine, sine, slot_len)
    positions = jnp.arange(row_count, dtype=jnp.int32) % slot_len
    valid = positions < jnp.repeat(reward_lengths, slot_len)
    reward_flat = jnp.where(valid[:, None], summed, 0).astype(jnp.bfloat16)

    last_index = reward_ids * slot_len + reward_lengths - 1
    last_rows = jnp.take(reward_flat, last_index, axis=0)
    last_float = last_rows.astype(jnp.float32)
    local_dots = jnp.dot(last_rows, w_score.T, preferred_element_type=jnp.float32)
    local_squares = jnp.sum(last_float * last_float, axis=1, keepdims=True)
    head_dots, square_sum = lax.psum((local_dots, local_squares), "tensor")
    reward_scores = head_dots * lax.rsqrt(square_sum / D + EPS)
    returning = jnp.dot(
        placing.T.astype(jnp.float32), reward_scores, precision=lax.Precision.HIGHEST
    ).reshape(n, CAP, OBJ)
    homecoming = lax.all_to_all(returning, "dp", split_axis=0, concat_axis=0, tiled=True)
    scores = jnp.dot(
        select.reshape(n * CAP, resp_dev).T.astype(jnp.float32),
        homecoming.reshape(n * CAP, OBJ),
        precision=lax.Precision.HIGHEST,
    )
    return (reward_flat.reshape(resp_dev, slot_len, width_part), scores)


def solution(mesh):
    in_specs = (
        P(("groups", "dp"), None, "tensor"),
        P("groups"),
        P("groups"),
        P(),
        P("dp", "tensor"),
        P(None, "dp", None),
        P("tensor", "dp"),
        P(None, "tensor"),
    )
    out_specs = (P(("groups", "dp"), None, "tensor"), P(("groups", "dp"), None))
    return jax.shard_map(body, mesh=mesh, in_specs=in_specs, out_specs=out_specs, check_vma=False)
```

time: 647 us -> 371 us (0.57)
  waiting for transfers between devices: 525 us -> 5.83 us
  Pallas kernels: 0 us -> 302 us
  matrix products: 51.3 us -> 1.12 us
  other arithmetic: 17.1 us -> 5.11 us
  between operations: 14 us -> 21 us
    all_gather x4 -> x0, waiting for transfers between devices: 355 us -> none  [the longest x1 147 us: body(): full_rows = lax.all_gather(local_rows, 'tensor', axis=1, tiled=True)]
    pallas_call x0 -> x1, Pallas kernels: none -> 302 us  [layer(): pl.pallas_call(functools.partial(kernel, (n, groups, count, slot_len)), o...]
    reduce_scatter x1 -> x0, waiting for transfers between devices: 143 us -> none  [body(): lax.psum_scatter(partial_value.astype(jnp.bfloat16), 'tensor', scatter_di...]
    dot_general x8 -> x1, matrix products: 51 us -> 0.78 us  [body(): jnp.dot(select.reshape(n * CAP, resp_dev).T.astype(jnp.float32), homecomi...]
    all_to_all x1 -> x0, waiting for transfers between devices: 25.4 us -> none  [body(): lax.all_to_all(outgoing.reshape(dp_count, CAP, slot_len * width_part), 'd...]
    reshape x4 -> x2, local copies, waits for them, and re-layouts: 7.32 us -> 0.82 us  [the longest x1 0.74 us: body(): route_table = route.reshape(n, resp_dev)]
  transfers between devices with their start and end apart: 6 -> 3, of which waited for: 6 -> 1; matrix products, arithmetic and copies ran while one was open for 7% -> 3% of each run, Pallas kernels for 0% -> 0%
where the time goes in v2:
time: 371 us; the launch traced here: 370 us
  Pallas kernels  302 us (81%)
  between operations  21 us (6%)
  local copies, waits for them, and re-layouts  15.5 us (4%)
  blocking collectives  15.1 us (4%)
  waiting for transfers between devices  5.83 us (2%)
  other arithmetic  5.11 us (1%)
  starting transfers between devices  4.57 us (1%)
    pallas_call x1, Pallas kernels, layer(): pl.pallas_call(functools.partial(kernel, (n, groups, count, slot_len)), o...  302 us
    psum x1, blocking collectives, body(): head_dots, square_sum = lax.psum((local_dots, local_squares), 'tensor')  8.98 us
  transfers between devices with their start and end apart: 3, of which 1 were waited for; matrix products, arithmetic and copies ran while one was open for 3% of the time, Pallas kernels for 0%

profile of v2, /device:TPU:0, one launch (start us, length us, event | category | flops | bytes accessed | tf_op | source)
XLA Modules:
  0.0 370.1 jit_solution(8001525469491207171)
XLA Ops:
  0.6 0.0 copy-start
  0.7 0.7 reshape.265
  1.4 0.2 convert_reduce_fusion
  1.7 0.1 fusion.5
  1.8 0.7 constant_dynamic-slice_fusion.2
  17.6 1.7 constant_dynamic-slice_fusion.1
  19.3 0.0 copy-start.2
  19.3 0.0 copy-start.3
  19.3 0.1 pad_maximum_fusion
  19.4 0.5 collective-permute-start
  19.9 0.1 pad_maximum_fusion.1
  19.9 2.6 collective-permute-start.1
  22.5 0.1 pad_maximum_fusion.2
  22.5 1.5 collective-permute-start.2
  24.0 0.1 convert_reduce_fusion.1
  24.2 0.0 copy-done.2
  24.2 0.2 reduce-window.16
  24.4 0.7 fusion.23
  26.3 0.1 copy.15
  26.4 0.1 reduce-window.15
  26.5 0.1 add_reduce_fusion
  26.6 0.0 copy-done.3
  26.6 0.1 select_reduce_fusion
  26.7 0.1 broadcast_in_dim.78
  26.8 0.1 reshape.264
  26.9 2.3 dynamic-slice_bitcast_fusion.kv_hbm
  29.1 0.3 fusion
  29.5 0.1 fusion.9
  29.5 0.8 pad_maximum_fusion.3
  30.3 1.8 broadcast_in_dim.80
  32.1 0.8 maximum_dynamic-update-slice_fusion
  36.7 0.0 collective-permute-done
  36.7 1.9 constant_dynamic-update-slice_fusion.2
  38.7 0.0 collective-permute-done.1
  38.7 0.9 constant_dynamic-update-slice_fusion.1
  39.5 5.8 %collective-permute-done.2 = bf16[2,64,2048]{2,1,0:T(8,128)(2,1)S(1)} collective-permute-done((bf16[2,64,2048]{2,1,0:T(8,128)(2,1)S(1)}, bf16[2,64,2048]{2,1,0:T(8,128)(2,1)S(1)}, u32[]{:S(2)}, u32[]{:S(2)}) %collective-permute-start.2) | collective-permute-done | bytes 524320 | tf_op jit(solution)/shard_map/ppermute | solution.py:473
  45.3 0.8 constant_dynamic-update-slice_fusion
  46.2 3.2 slice.6
  49.3 301.9 %shard_map.95 = bf16[512,2048]{1,0:T(8,128)(2,1)} custom-call(bf16[512,2048]{1,0:T(8,128)(2,1)} %bitcast.40, bf16[2048,1024]{1,0:T(8,128)(2,1)} %wq_hbm.1, bf16[2048,256]{1,0:T(8,128)(2,1)} %dynamic-slice_bitcast_fusion.kv_hbm, bf16[1024,2048]{1,0:T(8,128)(2,1)} %wo_hbm.1, f32[1,8192]{1,0:T(1,128)} %bitcast.43, f32[128,128]{1,0:T(8,128)} %get-tuple-element.37.cos_ref, ...), custom_call_target="tpu_custom_call" | custom-call | flops 21474836480 | bytes 62914560 | tf_op jit(solution)/shard_map/pallas_call | solution.py:408
  351.2 1.8 broadcast_select_fusion
  353.1 0.0 copy-start.1
  353.1 0.6 gather_fusion
  353.6 0.2 multiply_reduce_fusion
  353.8 0.0 copy-done
  353.8 0.2 fusion.1
  354.0 9.0 %all-reduce = (f32[8,3]{0,1:T(4,128)S(1)}, f32[8,1]{0,1:T(1,128)S(1)}) all-reduce(f32[8,3]{0,1:T(4,128)S(1)} %fusion.1, f32[8,1]{0,1:T(1,128)S(1)} %bitcast.42), channel_id=1, replica_groups=mesh['groups'=2,'tensor'=4,'dp'=4] {'tensor'}, use_global_device_ids=true, to_apply=%region_6.7 | all-reduce | flops 32 | bytes 256 | tf_op jit(solution)/shard_map/psum | solution.py:505
  363.0 0.1 fusion.2
  363.2 6.1 %all_to_all.5 = f32[4,2,3]{2,1,0:T(2,128)S(1)} all-to-all(f32[4,2,3]{2,1,0:T(2,128)S(1)} %fusion.2), channel_id=1, replica_groups=mesh['groups'=2,'tensor'=4,'dp'=4] {'dp'}, dimensions={0} | all-to-all | bytes 192 | tf_op jit(solution)/shard_map/all_to_all | solution.py:510
  369.3 0.8 convolution_bitcast_fusion
  370.1 0.0 copy-done.1
  (14 shorter events, 0.1 us)
Async XLA Ops:
  0.6 353.2 %copy-start = (bf16[3,2048]{1,0:T(4,128)(2,1)S(1)}, bf16[3,2048]{1,0:T(4,128)(2,1)}, u32[]{:S(2)}) copy-start(bf16[3,2048]{1,0:T(4,128)(2,1)} %param.15) | copy-start | bytes 36868
  19.3 4.9 %copy-start.2 = (s32[32]{0:T(128)S(1)}, s32[32]{0:T(128)}, u32[]{:S(2)}) copy-start(s32[32]{0:T(128)} %param.10) | copy-start | bytes 388
  19.3 7.3 %copy-start.3 = (s32[32]{0:T(128)S(1)}, s32[32]{0:T(128)}, u32[]{:S(2)}) copy-start(s32[32]{0:T(128)} %param.9) | copy-start | bytes 388
  19.4 17.4 %collective-permute-start = (bf16[2,64,2048]{2,1,0:T(8,128)(2,1)S(1)}, bf16[2,64,2048]{2,1,0:T(8,128)(2,1)}, u32[]{:S(2)}, u32[]{:S(2)}) collective-permute-start(bf16[2,64,2048]{2,1,0:T(8,128)(2,1)S(1)} %pad_maximum_fusion), channel_id=1, source_target_pairs={{0,1},{1,2},{2,3},{3,0},{4,5},{5,6},{6,7},{7,4},{8,9},{9,10},{10,1... | collective-permute-start | bytes 1572872 | tf_op jit(solution)/shard_map/ppermute | solution.py:473
  19.9 18.7 %collective-permute-start.1 = (bf16[2,64,2048]{2,1,0:T(8,128)(2,1)S(1)}, bf16[2,64,2048]{2,1,0:T(8,128)(2,1)S(1)}, u32[]{:S(2)}, u32[]{:S(2)}) collective-permute-start(bf16[2,64,2048]{2,1,0:T(8,128)(2,1)S(1)} %pad_maximum_fusion.1), channel_id=1, source_target_pairs={{0,2},{1,3},{2,0},{3,1},{4,6},{5,7},{6,4},{7,5},{8,10},{9,11},{10,... | collective-permute-start | bytes 1572872 | tf_op jit(solution)/shard_map/ppermute | solution.py:473
  22.5 22.8 %collective-permute-start.2 = (bf16[2,64,2048]{2,1,0:T(8,128)(2,1)S(1)}, bf16[2,64,2048]{2,1,0:T(8,128)(2,1)S(1)}, u32[]{:S(2)}, u32[]{:S(2)}) collective-permute-start(bf16[2,64,2048]{2,1,0:T(8,128)(2,1)S(1)} %pad_maximum_fusion.2), channel_id=1, source_target_pairs={{0,3},{1,0},{2,1},{3,2},{4,7},{5,4},{6,5},{7,6},{8,11},{9,8},{10,9... | collective-permute-start | bytes 1572872 | tf_op jit(solution)/shard_map/ppermute | solution.py:473
  353.1 17.0 %copy-start.1 = (bf16[512,2048]{1,0:T(8,128)(2,1)}, bf16[512,2048]{1,0:T(8,128)(2,1)S(1)}, u32[]{:S(2)}) copy-start(bf16[512,2048]{1,0:T(8,128)(2,1)S(1)} %broadcast_select_fusion) | copy-start | bytes 6291460

commit v3 on v2

--- a/solution.py
+++ b/solution.py
@@ -112,7 +112,7 @@
             for o in range(1, groups):
                 y_copy(i, k, o).start()
             core_copy(i, k, 0).start()
-        x_start(i + 2)
+        x_start(i + 3)
 
     def y_event(i):
         for k in range(1, chips):
@@ -182,9 +182,11 @@
             place_of = t if upward else count - 1 - t
             slot = up_slot if upward else down_slot
 
-            @pl.when(place_of == 0)
-            def _():
-                sum_copy(c, s, upward, True).start()
+            if s == 0:
+                @pl.when(place_of == 0)
+                def _():
+                    for later in range(count - 1):
+                        sum_copy(c, later, upward, True).start()
 
             if s > 0:
                 @pl.when((place_of > 0) & (place_of <= s))
@@ -328,6 +330,7 @@
     early = 1 + WPIECES
     x_start(0)
     x_start(1)
+    x_start(2)
     gather_step(0, 1)
     for a in range(3):
         own_core(a).start()
@@ -362,31 +365,39 @@
                 if s <= (count - 1) // 2:
                     sum_step(c - 1, s)
         project(c, wq, queries, 256)
-        for s in range(2, count // 2 + 1):
-            gather_step(c + 2, s)
-        if c:
+        if c == 0:
+            hops = [(2, s) for s in range(2, count + 1)] + [(3, 1)]
+            for i in range(early + 1, total):
+                if i + 1 < total:
+                    x_event(i + 1)
+                if hops:
+                    gather_step(*hops.pop(0))
+                y_event(i)
+            for hop in hops:
+                gather_step(*hop)
+            attend()
+            for i in range(early, total):
+                c_event(i)
+        else:
+            for s in range(2, count // 2 + 1):
+                gather_step(c + 2, s)
             for s in range(1, count - 1):
                 if s > (count - 1) // 2:
                     sum_step(c - 1, s)
-        attend()
-        for s in range(count // 2 + 1, count):
-            gather_step(c + 2, s)
-        if c == 0:
-            for i in range(early + 1, total):
-                if i + 1 < total:
-                    x_event(i + 1)
-                y_event(i)
-            for i in range(early, total):
-                c_event(i)
+            attend()
+            for s in range(count // 2 + 1, count):
+                gather_step(c + 2, s)
         output(c)
         sum_step(c, 0)
         if c:
-            sum_end(c - 1)
-        gather_step(c + 2, count)
-        gather_step(c + 3, 1)
+            gather_step(c + 2, count)
+            gather_step(c + 3, 1)
+        if c > 1:
+            sum_end(c - 2)
     for s in range(1, count - 1):
         sum_step(chunks - 1, s)
-    sum_end(chunks - 1)
+    for c in range(max(chunks - 2, 0), chunks):
+        sum_end(c)
     for c in range(chunks):
         sum_sent(c)
         out_copy(c).wait()

time: 371 us -> 355 us (0.957)
  Pallas kernels: 302 us -> 287 us
    pallas_call x1, Pallas kernels: 302 us -> 287 us  [layer(): pl.pallas_call(functools.partial(kernel, (n, groups, count, slot_len)), o...]
where the time goes in v3:
time: 355 us; the launch traced here: 354 us
  Pallas kernels  287 us (81%)
  between operations  21 us (6%)
  local copies, waits for them, and re-layouts  15.5 us (4%)
  blocking collectives  14.5 us (4%)
  waiting for transfers between devices  5.83 us (2%)
  other arithmetic  5.11 us (1%)
  starting transfers between devices  4.57 us (1%)
    pallas_call x1, Pallas kernels, layer(): pl.pallas_call(functools.partial(kernel, (n, groups, count, slot_len)), o...  287 us
    psum x1, blocking collectives, body(): head_dots, square_sum = lax.psum((local_dots, local_squares), 'tensor')  8.35 us
  transfers between devices with their start and end apart: 3, of which 1 were waited for; matrix products, arithmetic and copies ran while one was open for 3% of the time, Pallas kernels for 0%

profile of v3, /device:TPU:0, one launch (start us, length us, event | category | flops | bytes accessed | tf_op | source)
XLA Modules:
  0.0 354.2 jit_solution(9905136207101159861)
XLA Ops:
  0.6 0.0 copy-start
  0.7 0.7 reshape.265
  1.4 0.2 convert_reduce_fusion
  1.7 0.1 fusion.5
  1.8 0.7 constant_dynamic-slice_fusion.2
  17.6 1.7 constant_dynamic-slice_fusion.1
  19.3 0.0 copy-start.2
  19.3 0.0 copy-start.3
  19.3 0.1 pad_maximum_fusion
  19.4 0.5 collective-permute-start
  19.9 0.1 pad_maximum_fusion.1
  19.9 2.6 collective-permute-start.1
  22.5 0.1 pad_maximum_fusion.2
  22.5 1.5 collective-permute-start.2
  24.0 0.1 convert_reduce_fusion.1
  24.2 0.0 copy-done.2
  24.2 0.2 reduce-window.16
  24.4 0.7 fusion.23
  26.3 0.1 copy.15
  26.4 0.1 reduce-window.15
  26.5 0.1 add_reduce_fusion
  26.6 0.0 copy-done.3
  26.6 0.1 select_reduce_fusion
  26.7 0.1 broadcast_in_dim.78
  26.8 0.1 reshape.264
  26.9 2.3 dynamic-slice_bitcast_fusion.kv_hbm
  29.1 0.3 fusion
  29.5 0.1 fusion.9
  29.5 0.8 pad_maximum_fusion.3
  30.3 1.8 broadcast_in_dim.80
  32.1 0.8 maximum_dynamic-update-slice_fusion
  36.7 0.0 collective-permute-done
  36.7 1.9 constant_dynamic-update-slice_fusion.2
  38.7 0.0 collective-permute-done.1
  38.7 0.9 constant_dynamic-update-slice_fusion.1
  39.5 5.8 %collective-permute-done.2 = bf16[2,64,2048]{2,1,0:T(8,128)(2,1)S(1)} collective-permute-done((bf16[2,64,2048]{2,1,0:T(8,128)(2,1)S(1)}, bf16[2,64,2048]{2,1,0:T(8,128)(2,1)S(1)}, u32[]{:S(2)}, u32[]{:S(2)}) %collective-permute-start.2) | collective-permute-done | bytes 524320 | tf_op jit(solution)/shard_map/ppermute | solution.py:484
  45.3 0.8 constant_dynamic-update-slice_fusion
  46.2 3.2 slice.6
  49.3 286.7 %shard_map.95 = bf16[512,2048]{1,0:T(8,128)(2,1)} custom-call(bf16[512,2048]{1,0:T(8,128)(2,1)} %bitcast.40, bf16[2048,1024]{1,0:T(8,128)(2,1)} %wq_hbm.1, bf16[2048,256]{1,0:T(8,128)(2,1)} %dynamic-slice_bitcast_fusion.kv_hbm, bf16[1024,2048]{1,0:T(8,128)(2,1)} %wo_hbm.1, f32[1,8192]{1,0:T(1,128)} %bitcast.43, f32[128,128]{1,0:T(8,128)} %get-tuple-element.37.cos_ref, ...), custom_call_target="tpu_custom_call" | custom-call | flops 21474836480 | bytes 62914560 | tf_op jit(solution)/shard_map/pallas_call | solution.py:419
  336.0 1.8 broadcast_select_fusion
  337.8 0.0 copy-start.1
  337.8 0.6 gather_fusion
  338.4 0.2 multiply_reduce_fusion
  338.6 0.0 copy-done
  338.6 0.2 fusion.1
  338.8 8.3 %all-reduce = (f32[8,3]{0,1:T(4,128)S(1)}, f32[8,1]{0,1:T(1,128)S(1)}) all-reduce(f32[8,3]{0,1:T(4,128)S(1)} %fusion.1, f32[8,1]{0,1:T(1,128)S(1)} %bitcast.42), channel_id=1, replica_groups=mesh['groups'=2,'tensor'=4,'dp'=4] {'tensor'}, use_global_device_ids=true, to_apply=%region_6.7 | all-reduce | flops 32 | bytes 256 | tf_op jit(solution)/shard_map/psum | solution.py:516
  347.1 0.1 fusion.2
  347.3 6.1 %all_to_all.5 = f32[4,2,3]{2,1,0:T(2,128)S(1)} all-to-all(f32[4,2,3]{2,1,0:T(2,128)S(1)} %fusion.2), channel_id=1, replica_groups=mesh['groups'=2,'tensor'=4,'dp'=4] {'dp'}, dimensions={0} | all-to-all | bytes 192 | tf_op jit(solution)/shard_map/all_to_all | solution.py:521
  353.4 0.8 convolution_bitcast_fusion
  354.2 0.0 copy-done.1
  (14 shorter events, 0.1 us)
Async XLA Ops:
  0.6 338.0 %copy-start = (bf16[3,2048]{1,0:T(4,128)(2,1)S(1)}, bf16[3,2048]{1,0:T(4,128)(2,1)}, u32[]{:S(2)}) copy-start(bf16[3,2048]{1,0:T(4,128)(2,1)} %param.15) | copy-start | bytes 36868
  19.3 4.9 %copy-start.2 = (s32[32]{0:T(128)S(1)}, s32[32]{0:T(128)}, u32[]{:S(2)}) copy-start(s32[32]{0:T(128)} %param.10) | copy-start | bytes 388
  19.3 7.3 %copy-start.3 = (s32[32]{0:T(128)S(1)}, s32[32]{0:T(128)}, u32[]{:S(2)}) copy-start(s32[32]{0:T(128)} %param.9) | copy-start | bytes 388
  19.4 17.4 %collective-permute-start = (bf16[2,64,2048]{2,1,0:T(8,128)(2,1)S(1)}, bf16[2,64,2048]{2,1,0:T(8,128)(2,1)}, u32[]{:S(2)}, u32[]{:S(2)}) collective-permute-start(bf16[2,64,2048]{2,1,0:T(8,128)(2,1)S(1)} %pad_maximum_fusion), channel_id=1, source_target_pairs={{0,1},{1,2},{2,3},{3,0},{4,5},{5,6},{6,7},{7,4},{8,9},{9,10},{10,1... | collective-permute-start | bytes 1572872 | tf_op jit(solution)/shard_map/ppermute | solution.py:484
  19.9 18.7 %collective-permute-start.1 = (bf16[2,64,2048]{2,1,0:T(8,128)(2,1)S(1)}, bf16[2,64,2048]{2,1,0:T(8,128)(2,1)S(1)}, u32[]{:S(2)}, u32[]{:S(2)}) collective-permute-start(bf16[2,64,2048]{2,1,0:T(8,128)(2,1)S(1)} %pad_maximum_fusion.1), channel_id=1, source_target_pairs={{0,2},{1,3},{2,0},{3,1},{4,6},{5,7},{6,4},{7,5},{8,10},{9,11},{10,... | collective-permute-start | bytes 1572872 | tf_op jit(solution)/shard_map/ppermute | solution.py:484
  22.5 22.8 %collective-permute-start.2 = (bf16[2,64,2048]{2,1,0:T(8,128)(2,1)S(1)}, bf16[2,64,2048]{2,1,0:T(8,128)(2,1)S(1)}, u32[]{:S(2)}, u32[]{:S(2)}) collective-permute-start(bf16[2,64,2048]{2,1,0:T(8,128)(2,1)S(1)} %pad_maximum_fusion.2), channel_id=1, source_target_pairs={{0,3},{1,0},{2,1},{3,2},{4,7},{5,4},{6,5},{7,6},{8,11},{9,8},{10,9... | collective-permute-start | bytes 1572872 | tf_op jit(solution)/shard_map/ppermute | solution.py:484
  337.8 16.4 %copy-start.1 = (bf16[512,2048]{1,0:T(8,128)(2,1)}, bf16[512,2048]{1,0:T(8,128)(2,1)S(1)}, u32[]{:S(2)}) copy-start(bf16[512,2048]{1,0:T(8,128)(2,1)S(1)} %broadcast_select_fusion) | copy-start | bytes 6291460
